TPU v7x, 256 devices: a whole 4x4x8 slice. The times are simulated.
256 devices in a mesh: pool: 64 (over y, z, core), head: 4 (over x).
Axes of the slice: x: 4, y: 4, z: 8, core: 2. Of those that a mesh axis runs over, the one named last changes fastest.
Arguments:
- queries: bfloat16 [2048, 8192], P('pool', 'head'), may hold values from -16 to 16
- span_keys: bfloat16 [512, 512, 1024], P('pool', None, 'head'), may hold values from -7 to 7
- span_values: bfloat16 [512, 512, 1024], P('pool', None, 'head'), may hold values from -6 to 6
- span_ids: int32 [2048, 16], P('pool'), may hold values from 0 to 511, all different within a row; in each aligned block of 32 rows (0 to 31, 32 to 63, ...) at most 2 rows name the same one
- span_slot: int32 [512], replicated, may hold values from 0 to 511, each once
- out_weight: bfloat16 [8192, 5120], P('head', 'pool'), may hold values from -3 to 3
Outputs:
- mixed: bfloat16 [2048, 5120], P('pool', 'head')
Inputs may be any that keep to these rules, and one draw needn't show every extreme that they name: `span_ids`: each row names 16 different spans. Within the 32 requests of one index of pool, no span is named by more than 2 requests, a bound that some block reaches. `span_slot`: each storage position appears once.
All inputs are finite; a program needn't handle non-finite values.
Results may differ from a plain program's by a relative error of at most 0.015.
Values may be sent and summed in bfloat16 or wider, within the bound.
A program may use at most 128 MiB of HBM per device.

v0:
```python
import math

import jax
import jax.numpy as jnp
from jax import lax
from jax.sharding import PartitionSpec as P

HD = 128


def body(queries, span_keys, span_values, span_ids, span_slot, out_weight):
    req_rows, width = queries.shape
    picks = span_ids.shape[1]
    local_spans, span_len, kv_width = span_keys.shape
    head_size = HD
    kv_local = kv_width // head_size
    group = width // kv_width
    heads_local = kv_local * group
    owners = lax.axis_size("pool")
    spans_all = span_slot.shape[0]
    bucket = max(2, 2 * req_rows * picks // spans_all)
    pair_count = req_rows * picks
    flat_ids = span_ids.reshape(pair_count)
    matches = flat_ids[:, None] == jnp.arange(spans_all, dtype=jnp.int32)[None, :]
    slots = jnp.sum(jnp.where(matches, span_slot[None, :], 0), axis=1)
    ordinal = jnp.arange(pair_count, dtype=jnp.int32)
    earlier = (slots[:, None] == slots[None, :]) & (ordinal[:, None] > ordinal[None, :])
    ranking = jnp.sum(earlier, axis=1)
    owner_of = slots // local_spans
    local_of = slots % local_spans
    send_pos = slots * bucket + ranking
    outgoing = jnp.zeros((spans_all * bucket, width), jnp.bfloat16)
    outgoing = outgoing.at[send_pos].set(jnp.repeat(queries, picks, axis=0))
    outgoing = outgoing.reshape(owners, local_spans, bucket, width)
    incoming = lax.all_to_all(outgoing, "pool", split_axis=0, concat_axis=0, tiled=True)
    scale = 1.0 / math.sqrt(head_size)

    def attend(inputs):
        position, cache_keys, cache_values = inputs
        arrived = lax.dynamic_index_in_dim(incoming, position, 1, keepdims=False)
        query_block = arrived.reshape(owners, bucket, kv_local, group, head_size)
        key_block = cache_keys.reshape(span_len, kv_local, head_size)
        value_block = cache_values.reshape(span_len, kv_local, head_size)
        scores = (
            jnp.einsum(
                "nmkgd,tkd->nmkgt", query_block, key_block, preferred_element_type=jnp.float32
            )
            * scale
        )
        peaks = jnp.max(scores, axis=-1)
        expo = jnp.exp(scores - peaks[..., None])
        totals = jnp.sum(expo, axis=-1)
        partial_value = jnp.einsum(
            "nmkgt,tkd->nmkgd",
            expo.astype(jnp.bfloat16),
            value_block,
            preferred_element_type=jnp.float32,
        )
        partial_value = partial_value / totals[..., None]
        return (
            partial_value.astype(jnp.bfloat16).reshape(owners, bucket, width),
            peaks.reshape(owners, bucket, heads_local),
            totals.reshape(owners, bucket, heads_local),
        )

    partials, peak_parts, total_parts = lax.map(
        attend, (jnp.arange(local_spans, dtype=jnp.int32), span_keys, span_values)
    )
    returned = lax.all_to_all(partials, "pool", split_axis=1, concat_axis=1, tiled=True)
    peak_back, total_back = (
        lax.all_to_all(peak_parts, "pool", split_axis=1, concat_axis=1, tiled=True),
        lax.all_to_all(total_parts, "pool", split_axis=1, concat_axis=1, tiled=True),
    )
    fetch = local_of * (owners * bucket) + owner_of * bucket + ranking
    pieces = (
        returned.reshape(-1, width)[fetch]
        .reshape(req_rows, picks, heads_local, head_size)
        .astype(jnp.float32)
    )
    peak_pairs = peak_back.reshape(-1, heads_local)[fetch].reshape(req_rows, picks, heads_local)
    total_pairs = total_back.reshape(-1, heads_local)[fetch].reshape(req_rows, picks, heads_local)
    highest = jnp.max(peak_pairs, axis=1, keepdims=True)
    weights = jnp.exp(peak_pairs - highest) * total_pairs
    merged = jnp.sum(weights[..., None] * pieces, axis=1) / jnp.sum(weights, axis=1)[..., None]
    attention = merged.astype(jnp.bfloat16).reshape(req_rows, width)
    terms = jnp.dot(
        attention,
        lax.all_gather(out_weight, "pool", axis=1, tiled=True),
        preferred_element_type=jnp.float32,
    )
    return lax.psum_scatter(terms.astype(jnp.bfloat16), "head", scatter_dimension=1, tiled=True)


def solution(mesh):
    in_specs = (
        P("pool", "head"),
        P("pool", None, "head"),
        P("pool", None, "head"),
        P("pool", None),
        P(),
        P("head", "pool"),
    )
    out_specs = P("pool", "head")
    return jax.shard_map(body, mesh=mesh, in_specs=in_specs, out_specs=out_specs, check_vma=False)
```

profile of v0, /device:TPU:16, one launch (start us, length us, event | category | flops | bytes accessed | tf_op | source)
XLA Modules:
  0.0 486.1 jit_solution(8621826160981580448)
XLA Ops:
  10.5 6.2 %scatter_custom_fusion = bf16[1024,2048]{1,0:T(8,128)(2,1)} fusion(s32[512]{0:T(512)S(1)} %bitcast.105, bf16[512,2048]{1,0:T(8,128)(2,1)S(1)} %bitcast.96, bf16[]{:T(256)} %constant.57.clone.1), kind=kCustom, calls=%fused_computation.29 | custom fusion | bytes 4194306 | tf_op jit(solution)/shard_map/scatter | solution.py:33
  16.7 7.7 %reshape.183 = bf16[64,8,2,2048]{3,2,1,0:T(2,128)(2,1)} reshape(bf16[1024,2048]{1,0:T(8,128)(2,1)} %scatter_custom_fusion) | data formatting | bytes 8388608 | tf_op jit(solution)/shard_map/reshape | solution.py:34
  24.4 12.3 %all-to-all-start = ((bf16[64,8,2,2048]{3,2,1,0:T(2,128)(2,1)}), bf16[64,8,2,2048]{3,2,1,0:T(2,128)(2,1)}, u32[]{:S(2)}, u32[]{:S(2)}) async-start(bf16[64,8,2,2048]{3,2,1,0:T(2,128)(2,1)} %reshape.183), calls=%async_computation | async-start | bytes 8388608 | tf_op jit(solution)/shard_map/all_to_all | solution.py:35
  36.7 128.0 %all-to-all-done = bf16[64,8,2,2048]{3,2,1,0:T(2,128)(2,1)} async-done(((bf16[64,8,2,2048]{3,2,1,0:T(2,128)(2,1)}), bf16[64,8,2,2048]{3,2,1,0:T(2,128)(2,1)}, u32[]{:S(2)}, u32[]{:S(2)}) %all-to-all-start) | async-done | bytes 4194336 | tf_op jit(solution)/shard_map/all_to_all | solution.py:35
  164.7 123.8 %while.14 = (s32[]{:T(128)}, bf16[8,64,2,2048]{3,2,0,1:T(2,128)(2,1)}, f32[8,64,2,16]{1,3,2,0:T(8,128)S(1)}, f32[8,64,2,16]{1,3,2,0:T(8,128)S(1)}, bf16[8,512,25...) while((s32[]{:T(128)}, ...), condition=%wide.region_6.7_spmd, body=%wide.region_3.6_spmd.sunk | while | flops 545779712 | bytes 38380228 | solution.py:66
  170.9 2.0 copy-done
  175.3 3.3 fusion.46
  186.4 2.0 copy-done
  190.9 3.2 fusion.46
  201.9 2.0 copy-done
  206.3 3.2 fusion.46
  217.3 2.0 copy-done
  221.8 3.2 fusion.46
  232.8 2.0 copy-done
  237.2 3.2 fusion.46
  248.2 2.0 copy-done
  252.7 3.2 fusion.46
  263.7 2.0 copy-done
  268.1 3.2 fusion.46
  279.1 2.0 copy-done
  283.5 3.2 fusion.46
  289.6 8.7 %all-to-all-start.1 = ((f32[64,1,256]{2,1,0:T(1,128)}), f32[64,1,256]{2,1,0:T(1,128)S(1)}, u32[]{:S(2)}, u32[]{:S(2)}) async-start(f32[64,1,256]{2,1,0:T(1,128)} %reshape.230), calls=%async_computation.1 | async-start | bytes 131072 | tf_op jit(solution)/shard_map/all_to_all | solution.py:71
  298.9 7.5 %all-to-all-done.1 = f32[64,1,256]{2,1,0:T(1,128)S(1)} async-done(((f32[64,1,256]{2,1,0:T(1,128)}), f32[64,1,256]{2,1,0:T(1,128)S(1)}, u32[]{:S(2)}, u32[]{:S(2)}) %all-to-all-start.1) | async-done | bytes 65568 | tf_op jit(solution)/shard_map/all_to_all | solution.py:71
  306.4 13.6 %all_to_all.20 = f32[64,1,256]{2,1,0:T(1,128)S(1)} all-to-all(f32[64,1,256]{2,1,0:T(1,128)S(1)} %reshape.228), channel_id=1, replica_groups=mesh['pool'=64,'head'=4] {'pool'}, dimensions={0} | all-to-all | bytes 131072 | tf_op jit(solution)/shard_map/all_to_all | solution.py:72
  320.0 7.3 %all-to-all-start.3 = ((bf16[8,64,2,2048]{3,2,0,1:T(2,128)(2,1)}), bf16[8,64,2,2048]{3,2,0,1:T(2,128)(2,1)}, u32[]{:S(2)}, u32[]{:S(2)}) async-start(bf16[8,64,2,2048]{3,2,0,1:T(2,128)(2,1)} %get-tuple-element.51), calls=%async_computation.3 | async-start | bytes 8388608 | tf_op jit(solution)/shard_map/all_to_all | solution.py:69
  333.9 86.3 %all-to-all-done.3 = bf16[8,64,2,2048]{3,2,0,1:T(2,128)(2,1)} async-done(((bf16[8,64,2,2048]{3,2,0,1:T(2,128)(2,1)}), bf16[8,64,2,2048]{3,2,0,1:T(2,128)(2,1)}, u32[]{:S(2)}, u32[]{:S(2)}) %all-to-all-start.3) | async-done | bytes 4194336 | tf_op jit(solution)/shard_map/all_to_all | solution.py:69
  420.2 7.6 %copy.83 = bf16[8,64,2,2048]{3,2,1,0:T(2,128)(2,1)} copy(bf16[8,64,2,2048]{3,2,0,1:T(2,128)(2,1)} %all-to-all-done.3) | data formatting | bytes 8388608 | tf_op jit(solution)/shard_map/all_to_all | solution.py:69
  427.9 7.2 %reshape.188 = bf16[1024,2048]{1,0:T(8,128)(2,1)} reshape(bf16[8,64,2,2048]{3,2,1,0:T(2,128)(2,1)} %copy.83) | data formatting | bytes 8388608 | tf_op jit(solution)/shard_map/reshape | solution.py:76
  435.1 7.1 %gather_fusion.2 = bf16[512,2048]{1,0:T(8,128)(2,1)S(1)} fusion(bf16[1024,2048]{1,0:T(8,128)(2,1)} %reshape.188, s32[1024]{0:T(1024)S(1)} %pad_clamp_fusion), kind=kCustom, calls=%fused_computation.2 | custom fusion | bytes 4196352 | tf_op jit(solution)/shard_map/gather | solution.py:76
  443.7 1.4 fusion.20
  445.3 11.1 %convolution_convert_fusion = bf16[32,5120]{1,0:T(8,128)(2,1)} fusion(bf16[2048,5120]{0,1:T(8,128)(2,1)} %all-gather.2.cloned.1.call-done, bf16[4,8,16,128]{3,2,1,0:T(8,128)(2,1)S(1)} %bitcast.101), kind=kOutput, calls=%fused_computation.25 | convolution fusion | flops 671252480 | bytes 21430272 | tf_op jit(solution)/shard_map/dot_general | solution.py:86
  456.4 22.9 %reduce-scatter.2.cloned.1.call-done = bf16[32,1280]{1,0:T(8,128)(2,1)} async-done(((bf16[32,5120]{1,0:T(8,128)(2,1)}), bf16[32,1280]{1,0:T(8,128)(2,1)}) %reduce-scatter.2.cloned.1.call-update) | async-done | bytes 81936 | tf_op jit(solution)/shard_map/reduce_scatter | solution.py:91
  (145 shorter events, 80.4 us)
Async XLA Ops:
  6.5 438.7 %all-gather.2.cloned.1.call-start = ((), (), s32[]{:S(2)}) async-start(), calls=%async_computation.5 | async-start | bytes 21299200 | tf_op jit(solution)/shard_map/all_gather | solution.py:88
  24.4 140.3 %all-to-all-start = ((bf16[64,8,2,2048]{3,2,1,0:T(2,128)(2,1)}), bf16[64,8,2,2048]{3,2,1,0:T(2,128)(2,1)}, u32[]{:S(2)}, u32[]{:S(2)}) async-start(bf16[64,8,2,2048]{3,2,1,0:T(2,128)(2,1)} %reshape.183), calls=%async_computation | async-start | bytes 8388608 | tf_op jit(solution)/shard_map/all_to_all | solution.py:35
  170.9 2.0 copy-start
  186.4 2.0 copy-start
  201.9 2.0 copy-start
  217.3 2.0 copy-start
  232.8 2.0 copy-start
  248.2 2.0 copy-start
  263.7 2.0 copy-start
  279.1 2.0 copy-start
  289.6 16.7 %all-to-all-start.1 = ((f32[64,1,256]{2,1,0:T(1,128)}), f32[64,1,256]{2,1,0:T(1,128)S(1)}, u32[]{:S(2)}, u32[]{:S(2)}) async-start(f32[64,1,256]{2,1,0:T(1,128)} %reshape.230), calls=%async_computation.1 | async-start | bytes 131072 | tf_op jit(solution)/shard_map/all_to_all | solution.py:71
  320.0 100.2 %all-to-all-start.3 = ((bf16[8,64,2,2048]{3,2,0,1:T(2,128)(2,1)}), bf16[8,64,2,2048]{3,2,0,1:T(2,128)(2,1)}, u32[]{:S(2)}, u32[]{:S(2)}) async-start(bf16[8,64,2,2048]{3,2,0,1:T(2,128)(2,1)} %get-tuple-element.51), calls=%async_computation.3 | async-start | bytes 8388608 | tf_op jit(solution)/shard_map/all_to_all | solution.py:69
  327.3 151.9 %reduce-scatter.2.cloned.1.call-start = ((), (), s32[]{:S(2)}) async-start(), calls=%async_computation.6 | async-start | bytes 409600 | tf_op jit(solution)/shard_map/reduce_scatter | solution.py:91
Sparse Core Ops, SparseCore 0:
  10.1 177.6 all-gather.1
  456.5 22.7 reduce-scatter.1
where the time goes:
time: 488 us; the launch traced here: 486 us
  waiting for transfers between devices  245 us (50%)
  local copies, waits for them, and re-layouts  110 us (23%)
  matrix products  43 us (9%)
  starting transfers between devices  28.6 us (6%)
  other arithmetic  16.5 us (3%)
  loops' own time  15.6 us (3%)
  blocking collectives  13.6 us (3%)
  between operations  13.6 us (3%)
    all_to_all x1, waiting for transfers between devices, body(): lax.all_to_all(outgoing, 'pool', split_axis=0, concat_axis=0, tiled=True)  128 us
    all_to_all x1, waiting for transfers between devices, body(): lax.all_to_all(partials, 'pool', split_axis=1, concat_axis=1, tiled=True)  86.3 us
    dot_general x8, matrix products, attend(): jnp.einsum('nmkgt,tkd->nmkgd', expo.astype(jnp.bfloat16), value_block, pr...  25.6 us
    reduce_scatter x1, waiting for transfers between devices, body(): lax.psum_scatter(terms.astype(jnp.bfloat16), 'head', scatter_dimension=1,...  22.9 us
    dynamic_slice x40, local copies, waits for them, and re-layouts, body(): lax.map(attend, (jnp.arange(local_spans, dtype=jnp.int32), span_keys, spa...  22.6 us
    while x16, local copies, waits for them, and re-layouts  15.8 us
    another operation x1, loops' own time, body(): lax.map(attend, (jnp.arange(local_spans, dtype=jnp.int32), span_keys, spa...  15.6 us
    all_to_all x1, blocking collectives, body(): lax.all_to_all(total_parts, 'pool', split_axis=1, concat_axis=1, tiled=True)  13.6 us
  transfers between devices with their start and end apart: 5, of which 4 were waited for; matrix products, arithmetic and copies ran while one was open for 29% of the time, Pallas kernels for 0%

commit v1 on v0

v1 whole, which is shorter than its diff:
```python
import functools
import math

import jax
import jax.numpy as jnp
from jax import lax
from jax.experimental import pallas as pl
from jax.experimental.pallas import tpu as pltpu
from jax.sharding import PartitionSpec as P

NY, NZ, NC = 4, 8, 2
HR = 16
HD = 128


def coords():
    p = lax.axis_index("pool")
    return p // (NZ * NC), (p // NC) % NZ, p % NC


def pid(y, z, c):
    return ((y % NY) * NZ + z % NZ) * NC + c


def greet(peers):
    barrier = pltpu.get_barrier_semaphore()
    for peer in peers:
        pl.semaphore_signal(barrier, inc=1, device_id={"pool": peer}, device_id_type=pl.DeviceIdType.MESH)
    pl.semaphore_wait(barrier, len(peers))


def gather_kernel(q_ref, qa_ref, qb_ref, own_sem, ay_s, ay_r, az_s, az_r, bz_s, bz_r, by_s, by_r, bf_s, bf_r, sa_s, sa_r, sb_s, sb_r):
    y, z, c = coords()
    zu, zd = (z + 1) % NZ, (z + NZ - 1) % NZ
    yu, yd = (y + 1) % NY, (y + NY - 1) % NY
    sib = pid(y, z, 1 - c)
    greet([pid(y + 1, z, c), pid(y + 2, z, c), pid(y + 3, z, c), pid(y, z + 1, c), pid(y, z + 7, c), sib])

    sends = []

    def send(src, dst, ss, rs, to):
        d = pltpu.make_async_remote_copy(src_ref=src, dst_ref=dst, send_sem=ss, recv_sem=rs, device_id={"pool": to}, device_id_type=pl.DeviceIdType.MESH)
        d.start()
        sends.append(d)

    def arrived(dst, ss, rs):
        pltpu.make_async_remote_copy(src_ref=dst, dst_ref=dst, send_sem=ss, recv_sem=rs, device_id={"pool": sib}, device_id_type=pl.DeviceIdType.MESH).wait_recv()

    qa, qb = q_ref.at[0], q_ref.at[1]
    own_a = pltpu.make_async_copy(qa, qa_ref.at[c, z, y], own_sem.at[0])
    own_b = pltpu.make_async_copy(qb, qb_ref.at[c, y, z], own_sem.at[1])
    own_a.start()
    own_b.start()

    def b_z(k):
        up = qb if k == 1 else qb_ref.at[c, y, (z + NZ - (k - 1)) % NZ]
        dn = qb if k == 1 else qb_ref.at[c, y, (z + k - 1) % NZ]
        iu, idn = (z + NZ - (k - 1)) % NZ, (z + k - 1) % NZ
        if k < 4:
            send(up, qb_ref.at[c, y, iu], bz_s.at[2 * k - 2], bz_r.at[2 * k - 2], pid(y, zu, c))
            send(dn, qb_ref.at[c, y, idn], bz_s.at[2 * k - 1], bz_r.at[2 * k - 1], pid(y, zd, c))
        else:
            lo, hi = pl.ds(0, HR // 2), pl.ds(HR // 2, HR // 2)
            send(up.at[lo], qb_ref.at[c, y, iu, lo], bz_s.at[6], bz_r.at[6], pid(y, zu, c))
            send(dn.at[hi], qb_ref.at[c, y, idn, hi], bz_s.at[7], bz_r.at[7], pid(y, zd, c))

    def b_z_wait(k):
        iu, idn = (z + NZ - k) % NZ, (z + k) % NZ
        if k < 4:
            arrived(qb_ref.at[c, y, iu], bz_s.at[2 * k - 2], bz_r.at[2 * k - 2])
            arrived(qb_ref.at[c, y, idn], bz_s.at[2 * k - 1], bz_r.at[2 * k - 1])
        else:
            lo, hi = pl.ds(0, HR // 2), pl.ds(HR // 2, HR // 2)
            arrived(qb_ref.at[c, y, iu, lo], bz_s.at[6], bz_r.at[6])
            arrived(qb_ref.at[c, y, idn, hi], bz_s.at[7], bz_r.at[7])

    offs = [0, NZ - 1, 1, NZ - 2, 2, NZ - 3, 3, 4]

    def b_y(i):
        zz = (z + offs[i]) % NZ
        src = qb if i == 0 else qb_ref.at[c, y, zz]
        send(src, qb_ref.at[c, y, zz], by_s.at[2 * i], by_r.at[2 * i], pid(yu, z, c))
        send(src, qb_ref.at[c, y, zz], by_s.at[2 * i + 1], by_r.at[2 * i + 1], pid(yd, z, c))

    def b_f(i):
        zz = (z + offs[i]) % NZ
        arrived(qb_ref.at[c, yd, zz], by_s.at[2 * i], by_r.at[2 * i])
        arrived(qb_ref.at[c, yu, zz], by_s.at[2 * i + 1], by_r.at[2 * i + 1])
        lo, hi = pl.ds(0, HR // 2), pl.ds(HR // 2, HR // 2)
        send(qb_ref.at[c, yd, zz, lo], qb_ref.at[c, yd, zz, lo], bf_s.at[2 * i], bf_r.at[2 * i], pid(yu, z, c))
        send(qb_ref.at[c, yu, zz, hi], qb_ref.at[c, yu, zz, hi], bf_s.at[2 * i + 1], bf_r.at[2 * i + 1], pid(yd, z, c))

    def b_f_wait(i):
        zz = (z + offs[i]) % NZ
        lo, hi = pl.ds(0, HR // 2), pl.ds(HR // 2, HR // 2)
        yo = (y + 2) % NY
        arrived(qb_ref.at[c, yo, zz, lo], bf_s.at[2 * i], bf_r.at[2 * i])
        arrived(qb_ref.at[c, yo, zz, hi], bf_s.at[2 * i + 1], bf_r.at[2 * i + 1])

    jo = [0, 1, 3, 2]

    def a_z(k, j):
        yy = (y + jo[j]) % NY
        iu, idn = (z + NZ - (k - 1)) % NZ, (z + k - 1) % NZ
        up = qa if k == 1 and j == 0 else qa_ref.at[c, iu, yy]
        dn = qa if k == 1 and j == 0 else qa_ref.at[c, idn, yy]
        n = 8 * (k - 1) + 2 * j
        if k < 4 or j % 2 == 0:
            send(up, qa_ref.at[c, iu, yy], az_s.at[n], az_r.at[n], pid(y, zu, c))
        if k < 4 or j % 2 == 1:
            send(dn, qa_ref.at[c, idn, yy], az_s.at[n + 1], az_r.at[n + 1], pid(y, zd, c))

    def a_z_wait(k, j):
        yy = (y + jo[j]) % NY
        n = 8 * (k - 1) + 2 * j
        if k < 4 or j % 2 == 0:
            arrived(qa_ref.at[c, (z + NZ - k) % NZ, yy], az_s.at[n], az_r.at[n])
        if k < 4 or j % 2 == 1:
            arrived(qa_ref.at[c, (z + k) % NZ, yy], az_s.at[n + 1], az_r.at[n + 1])

    def s_a(i):
        zz = (z + offs[i]) % NZ
        send(qa_ref.at[c, zz], qa_ref.at[c, zz], sa_s.at[i], sa_r.at[i], sib)

    def s_b(j):
        yy = (y + j) % NY
        send(qb_ref.at[c, yy], qb_ref.at[c, yy], sb_s.at[j], sb_r.at[j], sib)

    b_z(1)
    for d in (1, 3, 2):
        send(qa, qa_ref.at[c, z, y], ay_s.at[d - 1], ay_r.at[d - 1], pid(y + d, z, c))
    a_z(1, 0)
    b_y(0)
    b_z_wait(1)
    b_z(2)
    b_y(1)
    b_y(2)
    for j in (1, 2, 3):
        d = (NY - jo[j]) % NY
        arrived(qa_ref.at[c, z, (y + jo[j]) % NY], ay_s.at[d - 1], ay_r.at[d - 1])
        a_z(1, j)
    own_a.wait()
    own_b.wait()
    s_a(0)
    b_f(0)
    for k in (1, 2, 3):
        b_z_wait(k + 1)
        if k < 3:
            b_z(k + 2)
        b_y(2 * k + 1)
        if k < 3:
            b_y(2 * k + 2)
        for j in range(4):
            a_z_wait(k, j)
            a_z(k + 1, j)
            if j == 1:
                b_f(2 * k - 1)
            if j == 3:
                b_f(2 * k)
        s_a(2 * k - 1)
        s_a(2 * k)
        if k == 3:
            s_b(0)
    b_f(7)
    s_b(1)
    s_b(3)
    for i in range(8):
        b_f_wait(i)
    s_b(2)
    for j in range(4):
        a_z_wait(4, j)
    s_a(7)
    for i in range(8):
        arrived(qa_ref.at[1 - c, (z + offs[i]) % NZ], sa_s.at[i], sa_r.at[i])
    for j in range(4):
        arrived(qb_ref.at[1 - c, (y + j) % NY], sb_s.at[j], sb_r.at[j])
    for d in sends:
        d.wait_send()


def gather_queries(q):
    dma = pltpu.SemaphoreType.DMA
    heads, hd = q.shape[1], q.shape[2]
    return pl.pallas_call(
        gather_kernel,
        out_shape=(
            jax.ShapeDtypeStruct((NC, NZ, NY, HR, heads, hd), q.dtype),
            jax.ShapeDtypeStruct((NC, NY, NZ, HR, heads, hd), q.dtype),
        ),
        in_specs=[pl.BlockSpec(memory_space=pl.ANY)],
        out_specs=(pl.BlockSpec(memory_space=pl.ANY),) * 2,
        scratch_shapes=[dma((2,)), dma((3,)), dma((3,)), dma((32,)), dma((32,)), dma((8,)), dma((8,)), dma((16,)), dma((16,)), dma((16,)), dma((16,)), dma((8,)), dma((8,)), dma((4,)), dma((4,))],
        compiler_params=pltpu.CompilerParams(collective_id=0, has_side_effects=True),
        name="gather_queries",
    )(q.reshape(2, HR, heads, hd))


NEG = -1e30
CHUNK = 32
ROWS = 2048
FLAG = 4096


def span_lists(ids_all, span_slot, local_spans):
    picks = ids_all.shape[-1]
    me = lax.axis_index("pool")
    mine = me * local_spans + jnp.arange(local_spans, dtype=jnp.int32)
    hit = span_slot[None, :] == mine[:, None]
    names = jnp.sum(jnp.where(hit, jnp.arange(span_slot.shape[0], dtype=jnp.int32)[None, :], 0), axis=1)
    member = jnp.any(ids_all[None] == names[:, None, None], axis=2).astype(jnp.float32)
    m = member.reshape(local_spans, NY, NZ, NC, 2, HR)
    first = m[:, :, :, :, 0].transpose(0, 3, 2, 1, 4).reshape(local_spans, -1)
    second = m[:, :, :, :, 1].transpose(0, 3, 1, 2, 4).reshape(local_spans, -1)
    m = jnp.concatenate([first, second], axis=1)
    parts = m.reshape(local_spans, ROWS // 128, 128)
    lane = jnp.arange(128)
    before = (lane[:, None] < lane[None, :]).astype(jnp.float32)
    within = jnp.einsum("sgl,lk->sgk", parts, before, preferred_element_type=jnp.float32)
    sums = jnp.sum(parts, axis=2)
    grp = jnp.arange(ROWS // 128)
    offset = jnp.sum(jnp.where(grp[None, :, None] > grp[None, None, :], sums[:, None, :], 0.0), axis=2)
    rank = (within + offset[:, :, None]).reshape(local_spans, ROWS).astype(jnp.int32)
    count = jnp.sum(sums, axis=1).astype(jnp.int32)
    span = jnp.arange(local_spans)
    prior = jnp.max(jnp.where(span[:, None, None] > span[None, :, None], m[None], 0.0), axis=1)
    place = jnp.arange(ROWS, dtype=jnp.int32)[None, :] + jnp.where(prior > 0, FLAG, 0)
    rank = jnp.where(m > 0, rank, -1)
    slot = jnp.arange(128, dtype=jnp.int32)
    listing = jnp.sum(jnp.where(rank[:, None, :] == slot[None, :, None], place[:, None, :], 0), axis=2)
    listing = jnp.where(slot[None, :] < count[:, None], listing, ROWS)
    return listing, count


def attend_kernel(list_ref, count_ref, qa_ref, qb_ref, k_ref, v_ref, da_ref, db_ref, st_ref, qbuf, dbuf, l0, l1, p0, p1, e0, e1, sem):
    s = pl.program_id(0)
    half = ROWS // 2

    @pl.when(s == 0)
    def _():
        ca = pltpu.make_async_copy(qa_ref, qbuf.at[pl.ds(0, half)], sem.at[0])
        cb = pltpu.make_async_copy(qb_ref, qbuf.at[pl.ds(half, half)], sem.at[1])
        ca.start()
        cb.start()

        def clear(i, _):
            dbuf[pl.ds(i * 16, 16)] = jnp.zeros((16, 16, 128), jnp.bfloat16)
            return 0

        lax.fori_loop(0, ROWS // 16, clear, 0)
        qbuf[pl.ds(ROWS, 8)] = jnp.zeros((8, 16, 128), jnp.bfloat16)
        st_ref[...] = jnp.full(st_ref.shape, NEG, jnp.float32)
        ca.wait()
        cb.wait()

    scale2 = math.log2(math.e) / math.sqrt(HD)
    lane = lax.broadcasted_iota(jnp.int32, (16, 128), 1)
    n = count_ref[s]

    def group_of(place):
        in_b = place >= half
        q = place - jnp.where(in_b, half, 0)
        g = jnp.where(in_b, 16 + q // 128, q // 64)
        return g, jnp.where(in_b, q % 128, q % 64)

    def chunk(j, _):
        base = j * CHUNK
        for i in range(0, CHUNK, 2):
            a = qbuf[list_ref[s, base + i] & (FLAG - 1)].astype(jnp.float32)
            b = qbuf[list_ref[s, base + i + 1] & (FLAG - 1)].astype(jnp.float32)
            l0[pl.ds(i * 8, 16)] = jnp.concatenate([a[0:8], b[0:8]], axis=0).astype(jnp.bfloat16)
            l1[pl.ds(i * 8, 16)] = jnp.concatenate([a[8:16], b[8:16]], axis=0).astype(jnp.bfloat16)
        for kv, (l, p, e) in enumerate(((l0, p0, e0), (l1, p1, e1))):
            keys = k_ref[0, :, kv * HD:(kv + 1) * HD]
            vals = v_ref[0, :, kv * HD:(kv + 1) * HD]
            sc = lax.dot_general(l[...], keys, (((1,), (1,)), ((), ())), preferred_element_type=jnp.float32) * scale2
            m = jnp.max(sc, axis=1, keepdims=True)
            ex = jnp.exp2(sc - m)
            tot = jnp.sum(ex, axis=1, keepdims=True)
            pv = jnp.dot(ex.astype(jnp.bfloat16), vals, preferred_element_type=jnp.float32)
            p[...] = pv / tot
            e[...] = jnp.broadcast_to(m + jnp.log2(tot), e.shape)
        for i in range(CHUNK):
            entry = list_ref[s, base + i]
            place = entry & (FLAG - 1)
            fresh = entry < FLAG
            new = jnp.concatenate([p0[pl.ds(i * 8, 8)], p1[pl.ds(i * 8, 8)]], axis=0)
            dbuf[jnp.where(fresh, place, ROWS)] = new.astype(jnp.bfloat16)
            g, at = group_of(jnp.minimum(place, ROWS - 1))
            at = jnp.where((entry < ROWS), at, -1)
            le = jnp.concatenate([e0[pl.ds(i * 8, 8)], e1[pl.ds(i * 8, 8)]], axis=0)
            st_ref[g] = jnp.where(lane == at, le, st_ref[g])

        def again(i, _):
            entry = list_ref[s, base + i]

            @pl.when(entry >= FLAG)
            def _():
                place = entry & (FLAG - 1)
                g, at = group_of(place)
                new = jnp.concatenate([p0[pl.ds(pl.multiple_of(i * 8, 8), 8)], p1[pl.ds(pl.multiple_of(i * 8, 8), 8)]], axis=0)
                le = jnp.concatenate([e0[pl.ds(pl.multiple_of(i * 8, 8), 8)], e1[pl.ds(pl.multiple_of(i * 8, 8), 8)]], axis=0)
                st = st_ref[g]
                old = jnp.max(jnp.where(lane == at, st, -3e38), axis=1, keepdims=True)
                top = jnp.maximum(old, le)
                wo, wn = jnp.exp2(old - top), jnp.exp2(le - top)
                both = wo + wn
                before = dbuf[place].astype(jnp.float32)
                dbuf[place] = (before + (wn / both) * (new - before)).astype(jnp.bfloat16)
                st_ref[g] = jnp.where(lane == at, top + jnp.log2(both), st)

            return 0

        lax.fori_loop(0, jnp.minimum(n - base, CHUNK), again, 0)
        return 0

    lax.fori_loop(0, (n + CHUNK - 1) // CHUNK, chunk, 0)

    @pl.when(s == pl.num_programs(0) - 1)
    def _():
        ca = pltpu.make_async_copy(dbuf.at[pl.ds(0, half)], da_ref, sem.at[0])
        cb = pltpu.make_async_copy(dbuf.at[pl.ds(half, half)], db_ref, sem.at[1])
        ca.start()
        cb.start()
        ca.wait()
        cb.wait()


def attend(listing, count, qa, qb, span_keys, span_values):
    spans, length, width = span_keys.shape
    half = ROWS // 2
    tile = jax.ShapeDtypeStruct((half, 16, HD), jnp.bfloat16)
    block = pl.BlockSpec((1, length, width), lambda s: (s, 0, 0))
    return pl.pallas_call(
        attend_kernel,
        grid=(spans,),
        out_shape=(tile, tile, jax.ShapeDtypeStruct((24, 16, 128), jnp.float32)),
        in_specs=[
            pl.BlockSpec(memory_space=pltpu.SMEM),
            pl.BlockSpec(memory_space=pltpu.SMEM),
            pl.BlockSpec(memory_space=pl.ANY),
            pl.BlockSpec(memory_space=pl.ANY),
            block,
            block,
        ],
        out_specs=(
            pl.BlockSpec(memory_space=pl.ANY),
            pl.BlockSpec(memory_space=pl.ANY),
            pl.BlockSpec((24, 16, 128), lambda s: (0, 0, 0)),
        ),
        scratch_shapes=[
            pltpu.VMEM((ROWS + 8, 16, HD), jnp.bfloat16),
            pltpu.VMEM((ROWS + 8, 16, HD), jnp.bfloat16),
            pltpu.VMEM((CHUNK * 8, HD), jnp.bfloat16),
            pltpu.VMEM((CHUNK * 8, HD), jnp.bfloat16),
            pltpu.VMEM((CHUNK * 8, HD), jnp.float32),
            pltpu.VMEM((CHUNK * 8, HD), jnp.float32),
            pltpu.VMEM((CHUNK * 8, HD), jnp.float32),
            pltpu.VMEM((CHUNK * 8, HD), jnp.float32),
            pltpu.SemaphoreType.DMA((2,)),
        ],
        compiler_params=pltpu.CompilerParams(vmem_limit_bytes=48 * 2**20, dimension_semantics=("arbitrary",)),
        name="attend",
    )(listing, count, qa.reshape(half, 16, HD), qb.reshape(half, 16, HD), span_keys, span_values)


def merge_kernel(da_ref, db_ref, sa_ref, sb_ref, out_ref,
                 ma, mb, ra, rb, sa, sb, rsa, rsb,
                 ua, da, usa, dsa, ub, db, usb, dsb, ya, ysa, uz, dz, usz, dsz,
                 own_sem, sib_s, sib_r, ua_s, ua_r, da_s, da_r, usa_s, usa_r, dsa_s, dsa_r,
                 ub_s, ub_r, db_s, db_r, usb_s, usb_r, dsb_s, dsb_r,
                 ya_s, ya_r, ysa_s, ysa_r, uz_s, uz_r, dz_s, dz_r, usz_s, usz_r, dsz_s, dsz_r):
    y, z, c = coords()
    zup, zdn = pid(y, z + 1, c), pid(y, z + NZ - 1, c)
    yup, ydn = pid(y + 1, z, c), pid(y + NY - 1, z, c)
    sib = pid(y, z, 1 - c)
    lane = lax.broadcasted_iota(jnp.int32, (16, 128), 1)

    loads = [
        pltpu.make_async_copy(da_ref.at[c], ma, own_sem.at[0]),
        pltpu.make_async_copy(db_ref.at[c], mb, own_sem.at[1]),
        pltpu.make_async_copy(sa_ref.at[c], sa, own_sem.at[2]),
        pltpu.make_async_copy(sb_ref.at[c], sb, own_sem.at[3]),
    ]
    for d in loads:
        d.start()
    greet([pid(y + 1, z, c), pid(y + 2, z, c), pid(y + 3, z, c), zup, zdn, sib])
    sends = []

    def send(src, dst, ss, rs, to):
        d = pltpu.make_async_remote_copy(src_ref=src, dst_ref=dst, send_sem=ss, recv_sem=rs, device_id={"pool": to}, device_id_type=pl.DeviceIdType.MESH)
        d.start()
        sends.append(d)

    def arrived(dst, ss, rs):
        pltpu.make_async_remote_copy(src_ref=dst, dst_ref=dst, send_sem=ss, recv_sem=rs, device_id={"pool": sib}, device_id_type=pl.DeviceIdType.MESH).wait_recv()

    def zz(d):
        return (z + d + NZ) % NZ

    def yy(d):
        return (y + d + NY) % NY

    a_order = [4, 3, -3, 2, -2, 1, -1, 0]
    b_order = [2, 1, -1, 0]
    send(sa_ref.at[1 - c], rsa, sib_s.at[12], sib_r.at[12], sib)
    send(sb_ref.at[1 - c], rsb, sib_s.at[13], sib_r.at[13], sib)

    def sib_a(i):
        w = zz(a_order[i])
        send(da_ref.at[1 - c, w], ra.at[w], sib_s.at[i], sib_r.at[i], sib)

    def sib_b(i):
        w = yy(b_order[i])
        send(db_ref.at[1 - c, w], rb.at[w], sib_s.at[8 + i], sib_r.at[8 + i], sib)

    sib_a(0)
    sib_b(0)
    sib_a(1)
    sib_a(2)
    sib_b(1)
    sib_b(2)
    sib_a(3)
    sib_a(4)
    sib_a(5)
    sib_a(6)
    sib_b(3)
    sib_a(7)

    def blend(dst, src, wt, rows=HR, start=0):
        for i in range(start, start + rows):
            w = jnp.broadcast_to(wt[:, i:i + 1], (16, 128))
            a = dst[i].astype(jnp.float32)
            b = src[i].astype(jnp.float32)
            dst[i] = (a + w * (b - a)).astype(jnp.bfloat16)

    def join(own, other):
        top = jnp.maximum(own, other)
        low = jnp.minimum(own, other)
        new = top + jnp.log2(1.0 + jnp.exp2(low - top))
        return new, jnp.exp2(other - new)

    def turned(wt, by):
        return pltpu.roll(wt, (128 - by) % 128, 1)

    for d in loads:
        d.wait()
    arrived(rsa, sib_s.at[12], sib_r.at[12])
    arrived(rsb, sib_s.at[13], sib_r.at[13])

    def core_a(i):
        w = zz(a_order[i])
        arrived(ra.at[w], sib_s.at[i], sib_r.at[i])
        new, wt = join(sa[w], rsa[w])
        sa[w] = new

        def cell(j, wt):
            blend(ma.at[w, j], ra.at[w, j], wt)
            return pltpu.roll(wt, 128 - HR, 1)

        lax.fori_loop(0, NY, cell, wt)

    def core_b(i):
        w = yy(b_order[i])
        arrived(rb.at[w], sib_s.at[8 + i], sib_r.at[8 + i])
        new, wt = join(sb[w], rsb[w])
        sb[w] = new

        def cell(j, wt):
            blend(mb.at[w, j], rb.at[w, j], wt)
            return pltpu.roll(wt, 128 - HR, 1)

        lax.fori_loop(0, NZ, cell, wt)

    def a_first():
        w = zz(4)
        st = sa[w]
        usa[4] = jnp.where(lane < 2 * HR, st, NEG)
        dsa[4] = jnp.where(lane < 2 * HR, NEG, st)
        send(usa.at[4], usa.at[0], usa_s.at[0], usa_r.at[0], zup)
        send(dsa.at[4], dsa.at[0], dsa_s.at[0], dsa_r.at[0], zdn)
        for j in (0, 1):
            send(ma.at[w, j], ua.at[0, j], ua_s.at[j], ua_r.at[j], zup)
            send(ma.at[w, 2 + j], da.at[0, 2 + j], da_s.at[2 + j], da_r.at[2 + j], zdn)

    def a_step(k):
        wu, wd = zz(4 - k), zz(k - 4)
        arrived(usa.at[k - 1], usa_s.at[k - 1], usa_r.at[k - 1])
        newu, wtu = join(sa[wu], usa[k - 1])
        sa[wu] = newu
        if k < 4:
            send(sa.at[wu], usa.at[k], usa_s.at[k], usa_r.at[k], zup)
        arrived(dsa.at[k - 1], dsa_s.at[k - 1], dsa_r.at[k - 1])
        newd, wtd = join(sa[wd], dsa[k - 1])
        sa[wd] = newd
        if k < 4:
            send(sa.at[wd], dsa.at[k], dsa_s.at[k], dsa_r.at[k], zdn)

        for j in range(NY):
            n = 4 * (k - 1) + j
            if k > 1 or j < 2:
                arrived(ua.at[k - 1, j], ua_s.at[n], ua_r.at[n])
                blend(ma.at[wu, j], ua.at[k - 1, j], turned(wtu, HR * j))
            if k < 4:
                send(ma.at[wu, j], ua.at[k, j], ua_s.at[n + 4], ua_r.at[n + 4], zup)
            if k > 1 or j >= 2:
                arrived(da.at[k - 1, j], da_s.at[n], da_r.at[n])
                blend(ma.at[wd, j], da.at[k - 1, j], turned(wtd, HR * j))
            if k < 4:
                send(ma.at[wd, j], da.at[k, j], da_s.at[n + 4], da_r.at[n + 4], zdn)

    def b_first():
        w = yy(2)
        st = sb[w]
        usb[2] = jnp.where(lane < 4 * HR, st, NEG)
        dsb[2] = jnp.where(lane < 4 * HR, NEG, st)
        send(usb.at[2], usb.at[0], usb_s.at[0], usb_r.at[0], yup)
        send(dsb.at[2], dsb.at[0], dsb_s.at[0], dsb_r.at[0], ydn)
        for j in range(4):
            send(mb.at[w, j], ub.at[0, j], ub_s.at[j], ub_r.at[j], yup)
            send(mb.at[w, 4 + j], db.at[0, 4 + j], db_s.at[4 + j], db_r.at[4 + j], ydn)

    def b_step(k):
        wu, wd = yy(2 - k), yy(k - 2)
        arrived(usb.at[k - 1], usb_s.at[k - 1], usb_r.at[k - 1])
        newu, wtu = join(sb[wu], usb[k - 1])
        sb[wu] = newu
        if k < 2:
            send(sb.at[wu], usb.at[k], usb_s.at[k], usb_r.at[k], yup)
        arrived(dsb.at[k - 1], dsb_s.at[k - 1], dsb_r.at[k - 1])
        newd, wtd = join(sb[wd], dsb[k - 1])
        sb[wd] = newd
        if k < 2:
            send(sb.at[wd], dsb.at[k], dsb_s.at[k], dsb_r.at[k], ydn)
        for j in range(NZ):
            n = 8 * (k - 1) + j
            if k > 1 or j < 4:
                arrived(ub.at[k - 1, j], ub_s.at[n], ub_r.at[n])
                blend(mb.at[wu, j], ub.at[k - 1, j], turned(wtu, HR * j))
            if k < 2:
                send(mb.at[wu, j], ub.at[k, j], ub_s.at[n + 8], ub_r.at[n + 8], yup)
            if k > 1 or j >= 4:
                arrived(db.at[k - 1, j], db_s.at[n], db_r.at[n])
                blend(mb.at[wd, j], db.at[k - 1, j], turned(wtd, HR * j))
            if k < 2:
                send(mb.at[wd, j], db.at[k, j], db_s.at[n + 8], db_r.at[n + 8], ydn)

    def a_y():
        for d in (1, 2, 3):
            w = yy(d)
            send(sa.at[z], ysa.at[d - 1], ysa_s.at[d - 1], ysa_r.at[d - 1], pid(y + d, z, c))
            send(ma.at[z, w], ya.at[d - 1], ya_s.at[d - 1], ya_r.at[d - 1], pid(y + d, z, c))

    def a_y_end():
        total = turned(sa[z], HR * y)
        for d in (1, 3, 2):
            arrived(ysa.at[d - 1], ysa_s.at[d - 1], ysa_r.at[d - 1])
            total, wt = join(total, turned(ysa[d - 1], HR * y))
            arrived(ya.at[d - 1], ya_s.at[d - 1], ya_r.at[d - 1])
            blend(ma.at[z, y], ya.at[d - 1], wt)

    def bz_first():
        w = zz(4)
        usz[4] = turned(sb[y], HR * w)
        send(usz.at[4], usz.at[0], usz_s.at[0], usz_r.at[0], zup)
        send(usz.at[4], dsz.at[0], dsz_s.at[0], dsz_r.at[0], zdn)
        lo, hi = pl.ds(0, HR // 2), pl.ds(HR // 2, HR // 2)
        send(mb.at[y, w, lo], uz.at[0, lo], uz_s.at[0], uz_r.at[0], zup)
        send(mb.at[y, w, hi], dz.at[0, hi], dz_s.at[0], dz_r.at[0], zdn)

    def bz_step(k):
        wu, wd = zz(4 - k), zz(k - 4)
        lo, hi = pl.ds(0, HR // 2), pl.ds(HR // 2, HR // 2)
        arrived(usz.at[k - 1], usz_s.at[k - 1], usz_r.at[k - 1])
        ru = usz[k - 1]
        if k == 1:
            ru = jnp.where(lane < HR // 2, ru, NEG)
        newu, wtu = join(turned(sb[y], HR * wu), ru)
        if k < 4:
            usz[4 + k] = newu
            send(usz.at[4 + k], usz.at[k], usz_s.at[k], usz_r.at[k], zup)
        arrived(dsz.at[k - 1], dsz_s.at[k - 1], dsz_r.at[k - 1])
        rd = dsz[k - 1]
        if k == 1:
            rd = jnp.where(lane < HR // 2, NEG, rd)
        own = turned(sb[y], HR * wd) if k < 4 else newu
        newd, wtd = join(own, rd)
        if k < 4:
            dsz[4 + k] = newd
            send(dsz.at[4 + k], dsz.at[k], dsz_s.at[k], dsz_r.at[k], zdn)
        if k == 1:
            arrived(uz.at[0, lo], uz_s.at[0], uz_r.at[0])
            blend(mb.at[y, wu], uz.at[0], wtu, HR // 2, 0)
        else:
            arrived(uz.at[k - 1], uz_s.at[k - 1], uz_r.at[k - 1])
            blend(mb.at[y, wu], uz.at[k - 1], wtu)
        if k < 4:
            send(mb.at[y, wu], uz.at[k], uz_s.at[k], uz_r.at[k], zup)
        if k == 1:
            arrived(dz.at[0, hi], dz_s.at[0], dz_r.at[0])
            blend(mb.at[y, wd], dz.at[0], wtd, HR // 2, HR // 2)
        else:
            arrived(dz.at[k - 1], dz_s.at[k - 1], dz_r.at[k - 1])
            blend(mb.at[y, wd], dz.at[k - 1], wtd)
        if k < 4:
            send(mb.at[y, wd], dz.at[k], dz_s.at[k], dz_r.at[k], zdn)

    core_a(0)
    a_first()
    core_b(0)
    b_first()
    core_a(1)
    core_a(2)
    a_step(1)
    core_b(1)
    core_b(2)
    b_step(1)
    core_a(3)
    core_a(4)
    a_step(2)
    core_a(5)
    core_a(6)
    a_step(3)
    core_b(3)
    b_step(2)
    bz_first()
    core_a(7)
    a_step(4)
    a_y()
    bz_step(1)
    bz_step(2)
    a_y_end()
    bz_step(3)
    bz_step(4)
    for d in sends:
        d.wait_send()
    out_ref[pl.ds(0, HR)] = ma[z, y]
    out_ref[pl.ds(HR, HR)] = mb[y, z]


def merge(da, db, st):
    dma = pltpu.SemaphoreType.DMA
    bf, f32 = jnp.bfloat16, jnp.float32

    def v(*shape, dtype=bf):
        return pltpu.VMEM(shape + (16, 128), dtype)

    anyspec = pl.BlockSpec(memory_space=pl.ANY)
    sems = [4, 14, 14, 16, 16, 16, 16, 4, 4, 4, 4, 16, 16, 16, 16, 2, 2, 2, 2, 3, 3, 3, 3, 4, 4, 4, 4, 4, 4, 4, 4]
    return pl.pallas_call(
        merge_kernel,
        out_shape=jax.ShapeDtypeStruct((2 * HR, 16, 128), bf),
        in_specs=[anyspec] * 4,
        out_specs=pl.BlockSpec(memory_space=pltpu.VMEM),
        scratch_shapes=[
            v(NZ, NY, HR), v(NY, NZ, HR), v(NZ, NY, HR), v(NY, NZ, HR),
            v(NZ, dtype=f32), v(NY, dtype=f32), v(NZ, dtype=f32), v(NY, dtype=f32),
            v(4, NY, HR), v(4, NY, HR), v(5, dtype=f32), v(5, dtype=f32),
            v(2, NZ, HR), v(2, NZ, HR), v(3, dtype=f32), v(3, dtype=f32),
            v(3, HR), v(3, dtype=f32),
            v(4, HR), v(4, HR), v(8, dtype=f32), v(8, dtype=f32),
        ] + [dma((n,)) for n in sems],
        compiler_params=pltpu.CompilerParams(collective_id=1, has_side_effects=True, vmem_limit_bytes=40 * 2**20),
        name="merge",
    )(
        da.reshape(NC, NZ, NY, HR, 16, 128),
        db.reshape(NC, NY, NZ, HR, 16, 128),
        st[:16].reshape(NC, NZ, 16, 128),
        st[16:].reshape(NC, NY, 16, 128),
    )


def body(queries, span_keys, span_values, span_ids, span_slot, out_weight):
    rows, width = queries.shape
    ids_all = lax.all_gather(span_ids, "pool", axis=0, tiled=True)
    zc = NZ * NC
    weight = lax.all_gather(out_weight.T, "pool", axis=0, tiled=True, axis_index_groups=[[y * zc + i for i in range(zc)] for y in range(NY)])
    qa, qb = gather_queries(queries.reshape(rows, width // HD, HD))
    listing, count = span_lists(ids_all, span_slot, span_keys.shape[0])
    da, db, st = attend(listing, count, qa, qb, span_keys, span_values)
    attention = merge(da, db, st).reshape(rows, width)
    near = lax.all_gather(attention, "pool", axis=0, tiled=True, axis_index_groups=[[y * zc + i for y in range(NY)] for i in range(zc)])
    terms = lax.dot_general(near, weight, (((1,), (1,)), ((), ())), preferred_element_type=jnp.float32)
    mine = lax.psum_scatter(terms.astype(jnp.bfloat16), "head", scatter_dimension=0, tiled=True)
    perm = []
    for y in range(NY):
        for i in range(zc):
            for x in range(4):
                perm.append(((y * zc + i) * 4 + x, (x * zc + i) * 4 + y))
    return lax.ppermute(mine, ("pool", "head"), perm)


def solution(mesh):
    in_specs = (
        P("pool", "head"),
        P("pool", None, "head"),
        P("pool", None, "head"),
        P("pool", None),
        P(),
        P("head", "pool"),
    )
    return jax.shard_map(body, mesh=mesh, in_specs=in_specs, out_specs=P("pool", "head"), check_vma=False)
```

time: 488 us -> 268 us (0.55)
  waiting for transfers between devices: 245 us -> 30.3 us
  Pallas kernels: 0 us -> 136 us
  local copies, waits for them, and re-layouts: 110 us -> 9.31 us
  blocking collectives: 13.6 us -> 65.5 us
  matrix products: 43 us -> 5.22 us
  starting transfers between devices: 28.6 us -> 3.37 us
  loops' own time: 15.6 us -> 0 us
  other arithmetic: 16.5 us -> 3.87 us
    all_to_all x3 -> x0, waiting for transfers between devices: 222 us -> none  [the longest x1 128 us: body(): lax.all_to_all(outgoing, 'pool', split_axis=0, concat_axis=0, tiled=True)]
    pallas_call x0 -> x3, Pallas kernels: none -> 136 us  [the longest x1 63.4 us: merge(): pl.pallas_call(merge_kernel, out_shape=jax.ShapeDtypeStruct((2 * HR, 16,...]
    all_gather x0 -> x2, blocking collectives: none -> 65.5 us  [the longest x1 52.8 us: body(): ids_all = lax.all_gather(span_ids, 'pool', axis=0, tiled=True)]
    dot_general x17 -> x2, matrix products: 43 us -> 5.22 us  [the longest x1 5.08 us: body(): lax.dot_general(near, weight, (((1,), (1,)), ((), ())), preferred_element...]
    dynamic_slice x48 -> x0, local copies, waits for them, and re-layouts: 33.9 us -> none  [the longest x40 22.6 us: body(): lax.map(attend, (jnp.arange(local_spans, dtype=jnp.int32), span_keys, spa...]
    all_to_all x3 -> x0, starting transfers between devices: 28.4 us -> none  [the longest x1 12.3 us: body(): lax.all_to_all(outgoing, 'pool', split_axis=0, concat_axis=0, tiled=True)]
    reshape x10 -> x0, local copies, waits for them, and re-layouts: 17.6 us -> none  [the longest x1 7.69 us: body(): outgoing = outgoing.reshape(owners, local_spans, bucket, width)]
    while x18 -> x0, local copies, waits for them, and re-layouts: 16.4 us -> none
  transfers between devices with their start and end apart: 5 -> 3, of which waited for: 4 -> 2; matrix products, arithmetic and copies ran while one was open for 29% -> 3% of each run, Pallas kernels for 0% -> 51%
where the time goes in v1:
time: 268 us; the launch traced here: 267 us
  Pallas kernels  136 us (51%)
  blocking collectives  65.5 us (24%)
  waiting for transfers between devices  30.3 us (11%)
  between operations  13.6 us (5%)
  local copies, waits for them, and re-layouts  9.31 us (3%)
  matrix products  5.22 us (2%)
  other arithmetic  3.87 us (1%)
  starting transfers between devices  3.37 us (1%)
    pallas_call x1, Pallas kernels, merge(): pl.pallas_call(merge_kernel, out_shape=jax.ShapeDtypeStruct((2 * HR, 16,...  63.4 us
    all_gather x1, blocking collectives, body(): ids_all = lax.all_gather(span_ids, 'pool', axis=0, tiled=True)  52.8 us
    pallas_call x1, Pallas kernels, attend(): pl.pallas_call(attend_kernel, grid=(spans,), out_shape=(tile, tile, jax.S...  36.8 us
    pallas_call x1, Pallas kernels, gather_queries(): pl.pallas_call(gather_kernel, out_shape=(jax.ShapeDtypeStruct((NC, NZ, NY...  36.2 us
    reduce_scatter x1, waiting for transfers between devices, body(): lax.psum_scatter(terms.astype(jnp.bfloat16), 'head', scatter_dimension=0,...  22.4 us
    all_gather x1, blocking collectives, body(): lax.all_gather(attention, 'pool', axis=0, tiled=True, axis_index_groups=[...  12.7 us
    unnamed x16, local copies, waits for them, and re-layouts  7.56 us
    ppermute x1, waiting for transfers between devices, body(): return lax.ppermute(mine, ('pool', 'head'), perm)  7.2 us
  transfers between devices with their start and end apart: 3, of which 2 were waited for; matrix products, arithmetic and copies ran while one was open for 3% of the time, Pallas kernels for 51%

profile of v1, /device:TPU:16, one launch (start us, length us, event | category | flops | bytes accessed | tf_op | source)
XLA Modules:
  0.0 267.5 jit_solution(1807214108735516271)
XLA Ops:
  6.5 0.7 all-gather.3.cloned.1.call-update
  7.3 52.8 %all-gather = s32[64,32,16]{1,2,0:T(8,128)S(1)} all-gather(s32[1,32,16]{1,2,0:T(8,128)} %bitcast.50), channel_id=1, replica_groups=mesh['pool'=64,'head'=4] {'pool'}, dimensions={0}, use_global_device_ids=true | all-gather | bytes 133120 | tf_op jit(solution)/shard_map/all_gather | solution.py:674
  60.1 0.2 copy.25
  60.3 0.2 reshape.120
  60.5 0.9 select_reduce_fusion.3
  61.4 0.3 compare_reduce_fusion
  61.7 0.7 reshape.118
  62.4 1.0 slice_reduce_fusion
  63.4 0.1 copy.26
  63.5 0.2 concatenate.21
  63.7 0.2 concatenate.18
  63.9 0.1 concatenate.22
  64.1 0.2 concatenate.19
  64.2 0.7 copy.31
  64.9 36.2 %gather_queries.1 = (bf16[2,8,4,16,16,128]{5,4,3,2,1,0:T(8,128)(2,1)}, bf16[2,4,8,16,16,128]{5,4,3,2,1,0:T(8,128)(2,1)}) custom-call(bf16[2,16,16,128]{3,2,1,0:T(8,128)(2,1)} %bitcast.47), custom_call_target="tpu_custom_call" | custom-call | tf_op jit(solution)/shard_map/gather_queries/pallas_call | solution.py:184
  101.1 0.1 reduce_sum.59
  101.3 0.1 select_reduce_fusion.2
  101.4 0.1 fusion.1
  101.5 0.2 select_reduce_fusion.1
  101.8 1.2 select_reduce_fusion
  103.0 0.1 fusion.4.list_ref
  103.1 1.6 copy-done.3
  104.7 36.8 %attend.1 = (bf16[1024,16,128]{2,1,0:T(8,128)(2,1)}, bf16[1024,16,128]{2,1,0:T(8,128)(2,1)}, f32[24,16,128]{2,1,0:T(8,128)S(1)}) custom-call(s32[8,128]{1,0:T(8,128)S(1)} %fusion.4.list_ref, s32[8]{0:T(128)S(1)} %add_convert_fusion.count_ref, bf16[1024,16,128]{2,1,0:T(8,128)(2,1)} %bitcast.42, bf16[1024,16,128]{2,1,0:T(8,128)(2,1)} %bitcast.43, ...), custom_call_target="tpu_custom_call" | custom-call | tf_op jit(solution)/shard_map/attend/pallas_call | solution.py:333
  141.5 2.2 copy-done
  143.7 2.2 copy-done.1
  145.9 63.4 %merge.1 = bf16[32,16,128]{2,1,0:T(8,128)(2,1)S(1)} custom-call(bf16[2,8,4,16,16,128]{5,4,3,2,1,0:T(8,128)(2,1)S(1)} %bitcast.37, bf16[2,4,8,16,16,128]{5,4,3,2,1,0:T(8,128)(2,1)S(1)} %bitcast.38, f32[2,8,16,128]{3,2,1,0:T(8,128)S(1)} %bitcast.39, f32[2,4,16,128]{3,2,1,0:T(8,128)S(1)} %bitcast.41), custom_call_target="tpu_custom_call" | custom-call | tf_op jit(solution)/shard_map/merge/pallas_call | solution.py:649
  209.3 12.7 %all_gather.10 = bf16[128,2048]{1,0:T(8,128)(2,1)S(1)} all-gather(bf16[32,2048]{1,0:T(8,128)(2,1)S(1)} %bitcast.46), channel_id=1, replica_groups={{0,64,128,192},{4,68,132,196},{8,72,136,200},{12,76,140,204},{16,80,144..., dimensions={0}, use_global_device_ids=true | all-gather | bytes 655360 | tf_op jit(solution)/shard_map/all_gather | solution.py:681
  222.0 5.1 %convolution_convert_fusion = bf16[128,1280]{1,0:T(8,128)(2,1)} fusion(bf16[128,2048]{1,0:T(8,128)(2,1)S(1)} %all_gather.10, bf16[1280,2048]{1,0:T(8,128)(2,1)} %all-gather.3.cloned.1.call-done), kind=kOutput, calls=%fused_computation.2 | convolution fusion | flops 671252480 | bytes 6094848 | tf_op jit(solution)/shard_map/dot_general | solution.py:682
  227.1 22.4 %reduce-scatter.2.cloned.1.call-done = bf16[32,1280]{1,0:T(8,128)(2,1)} async-done(((bf16[128,1280]{1,0:T(8,128)(2,1)}), bf16[32,1280]{1,0:T(8,128)(2,1)}) %reduce-scatter.2.cloned.1.call-update) | async-done | bytes 81936 | tf_op jit(solution)/shard_map/reduce_scatter | solution.py:683
  249.5 3.3 %collective-permute-start = (bf16[32,1280]{1,0:T(8,128)(2,1)}, bf16[32,1280]{1,0:T(8,128)(2,1)S(1)}, u32[]{:S(2)}, u32[]{:S(2)}) collective-permute-start(bf16[32,1280]{1,0:T(8,128)(2,1)} %reduce-scatter.2.cloned.1.call-done), channel_id=1, source_target_pairs={{0,0},{1,64},{2,128},{3,192},{4,4},{5,68},{6,132},{7,196},{8,8},{9... | collective-permute-start | bytes 245768 | tf_op jit(solution)/shard_map/ppermute | solution.py:689
  252.8 7.2 %collective-permute-done = bf16[32,1280]{1,0:T(8,128)(2,1)S(1)} collective-permute-done((bf16[32,1280]{1,0:T(8,128)(2,1)}, bf16[32,1280]{1,0:T(8,128)(2,1)S(1)}, u32[]{:S(2)}, u32[]{:S(2)}) %collective-permute-start) | collective-permute-done | bytes 81952 | tf_op jit(solution)/shard_map/ppermute | solution.py:689
  260.0 0.6 copy.39
  (25 shorter events, 0.2 us)
Async XLA Ops:
  6.5 57.7 %copy-start.4 = (bf16[32,2048]{1,0:T(8,128)(2,1)S(1)}, bf16[32,2048]{1,0:T(8,128)(2,1)}, u32[]{:S(2)}) copy-start(bf16[32,2048]{1,0:T(8,128)(2,1)} %param.6) | copy-start | bytes 393220
  6.5 96.6 %copy-start.2 = (bf16[8,512,256]{2,1,0:T(8,128)(2,1)S(1)}, bf16[8,512,256]{2,1,0:T(8,128)(2,1)}, u32[]{:S(2)}) copy-start(bf16[8,512,256]{2,1,0:T(8,128)(2,1)} %k_ref.1) | copy-start | bytes 6291460
  6.5 215.4 %all-gather.3.cloned.1.call-start = ((), (), s32[]{:S(2)}) async-start(), calls=%async_computation.1 | async-start | bytes 5570560 | tf_op jit(solution)/shard_map/all_gather | solution.py:676
  7.3 242.2 %reduce-scatter.2.cloned.1.call-start = ((), (), s32[]{:S(2)}) async-start(), calls=%async_computation.2 | async-start | bytes 409600 | tf_op jit(solution)/shard_map/reduce_scatter | solution.py:683
  103.1 1.6 copy-start.3
  141.5 2.2 copy-start
  143.7 2.2 copy-start.1
  249.5 10.5 %collective-permute-start = (bf16[32,1280]{1,0:T(8,128)(2,1)}, bf16[32,1280]{1,0:T(8,128)(2,1)S(1)}, u32[]{:S(2)}, u32[]{:S(2)}) collective-permute-start(bf16[32,1280]{1,0:T(8,128)(2,1)} %reduce-scatter.2.cloned.1.call-done), channel_id=1, source_target_pairs={{0,0},{1,64},{2,128},{3,192},{4,4},{5,68},{6,132},{7,196},{8,8},{9... | collective-permute-start | bytes 245768 | tf_op jit(solution)/shard_map/ppermute | solution.py:689
Sparse Core Ops, SparseCore 0:
  9.2 46.6 all-gather.2
  227.2 22.1 reduce-scatter.1

commit v2 on v1

v2 whole, which is shorter than its diff:
```python
import functools
import math

import jax
import jax.numpy as jnp
from jax import lax
from jax.experimental import pallas as pl
from jax.experimental.pallas import tpu as pltpu
from jax.sharding import PartitionSpec as P

NX, NY, NZ, NC = 4, 4, 8, 2
HR = 16
HD = 128
MESH = pl.DeviceIdType.MESH
OFFS = (0, NZ - 1, 1, NZ - 2, 2, NZ - 3, 3, 4)


def coords():
    p = lax.axis_index("pool")
    return p // (NZ * NC), (p // NC) % NZ, p % NC


def pid(y, z, c):
    return ((y % NY) * NZ + z % NZ) * NC + c


def gather_kernel(q_ref, w_ref, qs_ref, ws_ref, last_ref, own_sem, z_s, z_r, y_s, y_r, f_s, f_r, c_s, c_r, w_s, w_r, v_s, v_r):
    y, z, c = coords()
    zup, zdn = pid(y, z + 1, c), pid(y, z + NZ - 1, c)
    yu, yd = (y + 1) % NY, (y + NY - 1) % NY
    yup, ydn = pid(yu, z, c), pid(yd, z, c)
    sib = pid(y, z, 1 - c)
    barrier = pltpu.get_barrier_semaphore()
    for peer in (zup, zdn, yup, ydn, sib):
        pl.semaphore_signal(barrier, inc=1, device_id={"pool": peer}, device_id_type=MESH)
    pl.semaphore_wait(barrier, 5)
    sends = []

    def send(src, dst, ss, rs, to):
        d = pltpu.make_async_remote_copy(src_ref=src, dst_ref=dst, send_sem=ss, recv_sem=rs, device_id={"pool": to}, device_id_type=MESH)
        d.start()
        sends.append(d)

    def arrived(dst, ss, rs):
        pltpu.make_async_remote_copy(src_ref=dst, dst_ref=dst, send_sem=ss, recv_sem=rs, device_id={"pool": sib}, device_id_type=MESH).wait_recv()

    rows, wide = q_ref.shape[0], w_ref.shape[0]
    own_q = pltpu.make_async_copy(q_ref, qs_ref.at[c, y, z], own_sem.at[0])
    own_w = pltpu.make_async_copy(w_ref, ws_ref.at[z, c], own_sem.at[1])
    own_q.start()
    own_w.start()
    lo, hi = pl.ds(0, rows // 2), pl.ds(rows // 2, rows - rows // 2)
    wcut = wide // 32 * 16
    wlo, whi = pl.ds(0, wcut), pl.ds(wcut, wide - wcut)

    def q_z(k):
        iu, idn = (z + NZ - (k - 1)) % NZ, (z + k - 1) % NZ
        up = q_ref if k == 1 else qs_ref.at[c, y, iu]
        dn = q_ref if k == 1 else qs_ref.at[c, y, idn]
        if k < 4:
            send(up, qs_ref.at[c, y, iu], z_s.at[2 * k - 2], z_r.at[2 * k - 2], zup)
            send(dn, qs_ref.at[c, y, idn], z_s.at[2 * k - 1], z_r.at[2 * k - 1], zdn)
        else:
            send(up.at[lo], qs_ref.at[c, y, iu, lo], z_s.at[6], z_r.at[6], zup)
            send(dn.at[hi], qs_ref.at[c, y, idn, hi], z_s.at[7], z_r.at[7], zdn)

    def q_z_wait(k):
        iu, idn = (z + NZ - k) % NZ, (z + k) % NZ
        if k < 4:
            arrived(qs_ref.at[c, y, iu], z_s.at[2 * k - 2], z_r.at[2 * k - 2])
            arrived(qs_ref.at[c, y, idn], z_s.at[2 * k - 1], z_r.at[2 * k - 1])
        else:
            arrived(qs_ref.at[c, y, iu, lo], z_s.at[6], z_r.at[6])
            arrived(qs_ref.at[c, y, idn, hi], z_s.at[7], z_r.at[7])

    def w_z(k):
        iu, idn = (z + NZ - (k - 1)) % NZ, (z + k - 1) % NZ
        up = w_ref if k == 1 else ws_ref.at[iu, c]
        dn = w_ref if k == 1 else ws_ref.at[idn, c]
        if k < 4:
            send(up, ws_ref.at[iu, c], w_s.at[2 * k - 2], w_r.at[2 * k - 2], zup)
            send(dn, ws_ref.at[idn, c], w_s.at[2 * k - 1], w_r.at[2 * k - 1], zdn)
        else:
            send(up.at[wlo], ws_ref.at[iu, c, wlo], w_s.at[6], w_r.at[6], zup)
            send(dn.at[whi], ws_ref.at[idn, c, whi], w_s.at[7], w_r.at[7], zdn)

    def w_z_wait(k):
        iu, idn = (z + NZ - k) % NZ, (z + k) % NZ
        if k < 4:
            arrived(ws_ref.at[iu, c], w_s.at[2 * k - 2], w_r.at[2 * k - 2])
            arrived(ws_ref.at[idn, c], w_s.at[2 * k - 1], w_r.at[2 * k - 1])
        else:
            arrived(ws_ref.at[iu, c, wlo], w_s.at[6], w_r.at[6])
            arrived(ws_ref.at[idn, c, whi], w_s.at[7], w_r.at[7])

    def w_core(i):
        zz = (z + OFFS[i]) % NZ
        src = w_ref if i == 0 else ws_ref.at[zz, c]
        send(src, ws_ref.at[zz, c], v_s.at[i], v_r.at[i], sib)

    def q_core(j, i):
        yy, zz = (y + j) % NY, (z + OFFS[i]) % NZ
        src = q_ref if i == 0 and j == 0 else qs_ref.at[c, yy, zz]
        send(src, qs_ref.at[c, yy, zz], c_s.at[8 * j + i], c_r.at[8 * j + i], sib)

    def q_y(i):
        zz = (z + OFFS[i]) % NZ
        src = q_ref if i == 0 else qs_ref.at[c, y, zz]
        send(src, qs_ref.at[c, y, zz], y_s.at[2 * i], y_r.at[2 * i], yup)
        send(src, qs_ref.at[c, y, zz], y_s.at[2 * i + 1], y_r.at[2 * i + 1], ydn)
        q_core(0, i)

    def q_f(i):
        zz = (z + OFFS[i]) % NZ
        arrived(qs_ref.at[c, yd, zz], y_s.at[2 * i], y_r.at[2 * i])
        send(qs_ref.at[c, yd, zz, lo], qs_ref.at[c, yd, zz, lo], f_s.at[2 * i], f_r.at[2 * i], yup)
        arrived(qs_ref.at[c, yu, zz], y_s.at[2 * i + 1], y_r.at[2 * i + 1])
        send(qs_ref.at[c, yu, zz, hi], qs_ref.at[c, yu, zz, hi], f_s.at[2 * i + 1], f_r.at[2 * i + 1], ydn)
        q_core(1, i)
        q_core(3, i)

    def q_f_wait(i):
        zz, yo = (z + OFFS[i]) % NZ, (y + 2) % NY
        arrived(qs_ref.at[c, yo, zz, lo], f_s.at[2 * i], f_r.at[2 * i])
        arrived(qs_ref.at[c, yo, zz, hi], f_s.at[2 * i + 1], f_r.at[2 * i + 1])
        q_core(2, i)

    q_z(1)
    q_y(0)
    w_z(1)
    w_core(0)
    q_z_wait(1)
    q_z(2)
    q_y(1)
    q_y(2)
    q_f(0)
    q_z_wait(2)
    q_z(3)
    q_y(3)
    q_y(4)
    q_f(1)
    q_f(2)
    q_z_wait(3)
    q_z(4)
    q_y(5)
    q_y(6)
    w_z_wait(1)
    w_z(2)
    w_core(1)
    w_core(2)
    q_z_wait(4)
    q_y(7)
    q_f(3)
    q_f(4)
    w_z_wait(2)
    w_z(3)
    w_core(3)
    w_core(4)
    q_f(5)
    q_f(6)
    w_z_wait(3)
    w_z(4)
    w_core(5)
    w_core(6)
    q_f(7)
    for i in range(8):
        q_f_wait(i)
    w_z_wait(4)
    w_core(7)
    own_q.wait()
    own_w.wait()
    for i in range(8):
        zz = (z + OFFS[i]) % NZ
        arrived(ws_ref.at[zz, 1 - c], v_s.at[i], v_r.at[i])
        for j in range(4):
            arrived(qs_ref.at[1 - c, (y + j) % NY, zz], c_s.at[8 * j + i], c_r.at[8 * j + i])
    last = pltpu.make_async_copy(qs_ref.at[:, :, :, rows - 1], last_ref, own_sem.at[0])
    last.start()
    for d in sends:
        d.wait_send()
    last.wait()


def gather(q, wt):
    dma = pltpu.SemaphoreType.DMA
    anyspec = pl.BlockSpec(memory_space=pl.ANY)
    return pl.pallas_call(
        gather_kernel,
        out_shape=(
            pltpu.VMEM((NC, NY, NZ) + q.shape, q.dtype),
            pltpu.VMEM((NZ, NC) + wt.shape, wt.dtype),
            pltpu.VMEM((NC, NY, NZ) + q.shape[1:], q.dtype),
        ),
        in_specs=[anyspec] * 2,
        out_specs=(anyspec,) * 3,
        scratch_shapes=[dma((n,)) for n in (2, 8, 8, 16, 16, 16, 16, 32, 32, 8, 8, 8, 8)],
        compiler_params=pltpu.CompilerParams(collective_id=0, has_side_effects=True, vmem_limit_bytes=2**20),
        name="gather",
    )(q, wt)


NEG = -1e30
CHUNK = 32
BATCH = 8
ROWS = 2048
GROUPS = 24


def with_ids(queries, span_ids):
    flat = span_ids.T
    picks, rows = flat.shape
    tile = jnp.concatenate([flat // 32, flat % 32, jnp.zeros((picks, 128 - 2 * rows), jnp.int32)], axis=1)
    return jnp.concatenate([queries, tile.astype(queries.dtype)[None]], axis=0)


def list_requests(last_ref, slot_ref, first_ref, second_ref, lists_ref, counts_ref):
    spans = lists_ref.shape[0]
    me = lax.axis_index("pool")
    slots = slot_ref[...]
    where_id = lax.broadcasted_iota(jnp.int32, slots.shape, 0) * 128 + lax.broadcasted_iota(jnp.int32, slots.shape, 1)
    names = []
    for s in range(spans):
        found = jnp.where(slots == me * spans + s, where_id, 0).astype(jnp.float32)
        found = jnp.sum(found, axis=0, keepdims=True)
        names.append(jnp.broadcast_to(jnp.sum(found, axis=1, keepdims=True), (16, 128)))
    lane = lax.broadcasted_iota(jnp.int32, (8, 128), 1)
    sub = lax.broadcasted_iota(jnp.int32, (8, 128), 0)
    none = 1000

    def block(b, _):
        t = last_ref[b].astype(jnp.float32)
        ids = t * 32.0 + pltpu.roll(t, 96, 1)
        named = jnp.zeros((8, 128), jnp.float32)
        for s in range(spans):
            hit = jnp.where(ids == names[s], 1.0, 0.0)
            hit = jnp.max(hit, axis=0, keepdims=True)
            named = jnp.where(sub == s, jnp.broadcast_to(hit, (8, 128)), named)
        hit = (named > 0.0) & (lane < 32)
        low = jnp.min(jnp.where(hit, lane, none).astype(jnp.float32), axis=1, keepdims=True)
        high = jnp.max(jnp.where(hit, lane, -1).astype(jnp.float32), axis=1, keepdims=True)
        at = pl.ds(pl.multiple_of(b * 8, 8), 8)
        first_ref[at] = jnp.broadcast_to(low, (8, 128))
        second_ref[at] = jnp.broadcast_to(jnp.where(high > low, high, float(none)), (8, 128))
        return 0

    blocks = last_ref.shape[0]
    lax.fori_loop(0, blocks, block, 0, unroll=4)
    b = lax.broadcasted_iota(jnp.int32, (blocks, 128), 0)
    k = lax.broadcasted_iota(jnp.int32, (blocks, 128), 1).astype(jnp.float32)
    z, y, c = b % NZ, b // NZ % NY, b // (NZ * NY)
    early = c * 512 + (z * NY + y) * HR
    late = ROWS // 2 + c * 512 + (y * NZ + z) * HR - HR
    below = jnp.where(lax.broadcasted_iota(jnp.int32, (blocks, blocks), 0) > lax.broadcasted_iota(jnp.int32, (blocks, blocks), 1), 1.0, 0.0).astype(jnp.bfloat16)
    for s in range(spans):
        count = jnp.zeros((1, 128), jnp.float32)
        listing = jnp.zeros((1, 128), jnp.int32)
        for ref in (first_ref, second_ref):
            row = ref[pl.ds(s, blocks, stride=8), :]
            used = row < 32.0
            one = jnp.where(used, 1.0, 0.0)
            rank = jnp.dot(below, one.astype(jnp.bfloat16), preferred_element_type=jnp.float32) + count
            r = row.astype(jnp.int32)
            place = jnp.where(r < HR, early, late) + r + 4096 * (b * 33 + r)
            listing += jnp.sum(jnp.where(used & (rank == k), place, 0), axis=0, keepdims=True)
            count += jnp.sum(one, axis=0, keepdims=True)
        lists_ref[s:s + 1, :] = jnp.where(lane[0:1].astype(jnp.float32) < count, listing, ROWS)
        counts_ref[s:s + 1, :] = count.astype(jnp.int32)


def attend_kernel(last_ref, slot_ref, q_ref, k_hbm, v_hbm, d_ref, st_ref, first_ref, second_ref, lists_ref, counts_ref, list_ref, count_ref, lsem, kbuf, vbuf, l0, l1, p0, p1, e0, e1, ksem, vsem):
    spans = kbuf.shape[0]
    for s in range(spans):
        for hbm, buf, sem in ((k_hbm, kbuf, ksem), (v_hbm, vbuf, vsem)):
            d = pltpu.make_async_copy(hbm.at[s], buf.at[s], sem.at[s])
            d.start()

    list_requests(last_ref, slot_ref, first_ref, second_ref, lists_ref, counts_ref)
    moves = [pltpu.make_async_copy(lists_ref, list_ref, lsem.at[0]), pltpu.make_async_copy(counts_ref, count_ref, lsem.at[1])]
    for d in moves:
        d.start()

    def clear(i, _):
        d_ref[pl.ds(i * 8, 8)] = jnp.zeros((8, 16, 128), jnp.bfloat16)
        return 0

    lax.fori_loop(0, ROWS // 8 + 1, clear, 0)
    st_ref[...] = jnp.full(st_ref.shape, NEG, jnp.float32)
    for d in moves:
        d.wait()
    scale2 = math.log2(math.e) / math.sqrt(HD)
    lane = lax.broadcasted_iota(jnp.int32, (16, 128), 1)

    def span(s, _):
        pltpu.make_async_copy(k_hbm.at[s], kbuf.at[s], ksem.at[s]).wait()
        pltpu.make_async_copy(v_hbm.at[s], vbuf.at[s], vsem.at[s]).wait()
        n = count_ref[s, 0]

        def chunk(j, _):
            base = j * CHUNK
            for i in range(0, CHUNK, 2):
                a = q_ref[list_ref[s, base + i] >> 12].astype(jnp.float32)
                b = q_ref[list_ref[s, base + i + 1] >> 12].astype(jnp.float32)
                l0[pl.ds(i * 8, 16)] = jnp.concatenate([a[0:8], b[0:8]], axis=0).astype(jnp.bfloat16)
                l1[pl.ds(i * 8, 16)] = jnp.concatenate([a[8:16], b[8:16]], axis=0).astype(jnp.bfloat16)
            for kv, (l, p, e) in enumerate(((l0, p0, e0), (l1, p1, e1))):
                keys = kbuf[s, :, kv * HD:(kv + 1) * HD]
                vals = vbuf[s, :, kv * HD:(kv + 1) * HD]
                sc = lax.dot_general(l[...], keys, (((1,), (1,)), ((), ())), preferred_element_type=jnp.float32) * scale2
                m = jnp.max(sc, axis=1, keepdims=True)
                ex = jnp.exp2(sc - m)
                tot = jnp.sum(ex, axis=1, keepdims=True)
                pv = jnp.dot(ex.astype(jnp.bfloat16), vals, preferred_element_type=jnp.float32)
                p[...] = pv / tot
                e[...] = jnp.broadcast_to(m + jnp.log2(tot), e.shape)
            for first in range(0, CHUNK, BATCH):
                done = []
                for i in range(first, first + BATCH):
                    place = list_ref[s, base + i] & 4095
                    early = place < ROWS // 2
                    g = jnp.where(early, place >> 6, 8 + (place >> 7))
                    at = place & jnp.where(early, 63, 127)
                    here = lane == at
                    new = jnp.concatenate([p0[pl.ds(i * 8, 8)], p1[pl.ds(i * 8, 8)]], axis=0)
                    le = jnp.concatenate([e0[pl.ds(i * 8, 8)], e1[pl.ds(i * 8, 8)]], axis=0)
                    old = d_ref[place].astype(jnp.float32)
                    ol = jnp.max(jnp.where(here, st_ref[g], -3e38), axis=1, keepdims=True)
                    ex = jnp.exp2(-jnp.abs(le - ol))
                    both = 1.0 + ex
                    w = jnp.where(le > ol, 1.0, ex) / both
                    done.append((place, g, here, old + w * (new - old), jnp.maximum(le, ol) + jnp.log2(both)))
                for place, g, here, tile, le in done:
                    d_ref[place] = tile.astype(jnp.bfloat16)
                for place, g, here, tile, le in done:
                    st_ref[g] = jnp.where(here, le, st_ref[g])
            return 0

        lax.fori_loop(0, (n + CHUNK - 1) // CHUNK, chunk, 0)
        return 0

    lax.fori_loop(0, spans, span, 0)


def attend(last, span_slot, qs, span_keys, span_values):
    anyspec = pl.BlockSpec(memory_space=pl.ANY)
    vmem = pl.BlockSpec(memory_space=pltpu.VMEM)
    rows = CHUNK * 8
    spans = span_keys.shape[0]
    blocks = NC * NY * NZ
    return pl.pallas_call(
        attend_kernel,
        out_shape=(pltpu.VMEM((ROWS + 8, 16, HD), jnp.bfloat16), pltpu.VMEM((GROUPS + 1, 16, 128), jnp.float32)),
        in_specs=[vmem, vmem, vmem, anyspec, anyspec],
        out_specs=(vmem, vmem),
        scratch_shapes=[pltpu.VMEM((blocks * 8, 128), jnp.float32)] * 2
        + [pltpu.VMEM((spans, 128), jnp.int32)] * 2
        + [pltpu.SMEM((spans, 128), jnp.int32)] * 2
        + [pltpu.SemaphoreType.DMA((2,))]
        + [pltpu.VMEM(span_keys.shape, jnp.bfloat16)] * 2
        + [pltpu.VMEM((rows, HD), jnp.bfloat16)] * 2
        + [pltpu.VMEM((rows, HD), jnp.float32)] * 4
        + [pltpu.SemaphoreType.DMA((spans,))] * 2,
        compiler_params=pltpu.CompilerParams(vmem_limit_bytes=24 * 2**20),
        name="attend",
    )(
        last.reshape(blocks, 16, 128),
        span_slot.reshape(-1, 128),
        pltpu.with_memory_space_constraint(qs.reshape(-1, 16, HD), pltpu.VMEM),
        pltpu.with_memory_space_constraint(span_keys, pltpu.HBM),
        pltpu.with_memory_space_constraint(span_values, pltpu.HBM),
    )


def merge_kernel(d_ref, st_ref, w_ref, out_ref,
                 ma, mb, ra, rb, sa, sb, rsa, rsb,
                 ua, da, usa, dsa, ub, db, usb, dsb, ya, ysa, uz, dz, usz, dsz,
                 fa, near, terms, xin, tsum, fin,
                 n_s, n_r, t_s, t_r, g_s, g_r,
                 own_sem, sib_s, sib_r, ua_s, ua_r, da_s, da_r, usa_s, usa_r, dsa_s, dsa_r,
                 ub_s, ub_r, db_s, db_r, usb_s, usb_r, dsb_s, dsb_r,
                 ya_s, ya_r, ysa_s, ysa_r, uz_s, uz_r, dz_s, dz_r, usz_s, usz_r, dsz_s, dsz_r):
    y, z, c = coords()
    zup, zdn = pid(y, z + 1, c), pid(y, z + NZ - 1, c)
    yup, ydn = pid(y + 1, z, c), pid(y + NY - 1, z, c)
    sib = pid(y, z, 1 - c)
    lane = lax.broadcasted_iota(jnp.int32, (16, 128), 1)

    x = lax.axis_index("head")

    def d_a(core, w):
        return d_ref.at[pl.ds(core * 512 + w * (NY * HR), NY * HR)]

    def d_b(core, w):
        return d_ref.at[pl.ds(ROWS // 2 + core * 512 + w * (NZ * HR), NZ * HR)]

    loads = [
        pltpu.make_async_copy(st_ref.at[pl.ds(c * NZ, NZ)], sa, own_sem.at[0]),
        pltpu.make_async_copy(st_ref.at[pl.ds(2 * NZ + c * NY, NY)], sb, own_sem.at[1]),
    ]
    for d in loads:
        d.start()
    barrier = pltpu.get_barrier_semaphore()
    for peer in (pid(y + 1, z, c), pid(y + 2, z, c), pid(y + 3, z, c), zup, zdn, sib):
        pl.semaphore_signal(barrier, inc=1, device_id={"pool": peer, "head": x}, device_id_type=MESH)
    me = pid(y, z, c)
    for d in (1, 2, 3):
        pl.semaphore_signal(barrier, inc=1, device_id={"pool": me, "head": (x + d) % NX}, device_id_type=MESH)
    flip = {"pool": pid(x, z, c), "head": y}

    @pl.when(x != y)
    def _():
        pl.semaphore_signal(barrier, inc=1, device_id=flip, device_id_type=MESH)
        pl.semaphore_wait(barrier, 10)

    @pl.when(x == y)
    def _():
        pl.semaphore_wait(barrier, 9)

    sends = []

    def send(src, dst, ss, rs, to, head=x):
        d = pltpu.make_async_remote_copy(src_ref=src, dst_ref=dst, send_sem=ss, recv_sem=rs, device_id={"pool": to, "head": head}, device_id_type=MESH)
        d.start()
        sends.append(d)

    def arrived(dst, ss, rs):
        pltpu.make_async_remote_copy(src_ref=dst, dst_ref=dst, send_sem=ss, recv_sem=rs, device_id={"pool": sib}, device_id_type=MESH).wait_recv()

    def zz(d):
        return (z + d + NZ) % NZ

    def yy(d):
        return (y + d + NY) % NY

    a_order = [4, 3, -3, 2, -2, 1, -1, 0]
    b_order = [2, 1, -1, 0]
    send(st_ref.at[pl.ds((1 - c) * NZ, NZ)], rsa, sib_s.at[12], sib_r.at[12], sib)
    send(st_ref.at[pl.ds(2 * NZ + (1 - c) * NY, NY)], rsb, sib_s.at[13], sib_r.at[13], sib)

    def sib_a(i):
        w = zz(a_order[i])
        send(d_a(1 - c, w), ra.at[w], sib_s.at[i], sib_r.at[i], sib)

    def sib_b(i):
        w = yy(b_order[i])
        send(d_b(1 - c, w), rb.at[w], sib_s.at[8 + i], sib_r.at[8 + i], sib)

    sib_a(0)
    sib_b(0)
    sib_a(1)
    sib_a(2)
    sib_b(1)
    sib_b(2)
    sib_a(3)
    sib_a(4)
    sib_a(5)
    sib_a(6)
    sib_b(3)
    sib_a(7)

    def blend(dst, src, wt, rows=HR, start=0, base=None):
        base = dst if base is None else base
        for i in range(start, start + rows):
            w = jnp.broadcast_to(wt[:, i:i + 1], (16, 128))
            a = base[i].astype(jnp.float32)
            b = src[i].astype(jnp.float32)
            dst[i] = (a + w * (b - a)).astype(jnp.bfloat16)

    def join(own, other):
        top = jnp.maximum(own, other)
        low = jnp.minimum(own, other)
        new = top + jnp.log2(1.0 + jnp.exp2(low - top))
        return new, jnp.exp2(other - new)

    def turned(wt, by):
        return pltpu.roll(wt, (128 - by) % 128, 1)

    for d in loads:
        d.wait()
    arrived(rsa, sib_s.at[12], sib_r.at[12])
    arrived(rsb, sib_s.at[13], sib_r.at[13])

    def core_a(i):
        w = zz(a_order[i])
        arrived(ra.at[w], sib_s.at[i], sib_r.at[i])
        new, wt = join(sa[w], rsa[w])
        sa[w] = new

        def cell(j, wt):
            part = pl.ds(j * HR, HR)
            blend(ma.at[w, j], ra.at[w, part], wt, base=d_a(c, w).at[part])
            return pltpu.roll(wt, 128 - HR, 1)

        lax.fori_loop(0, NY, cell, wt)

    def core_b(i):
        w = yy(b_order[i])
        arrived(rb.at[w], sib_s.at[8 + i], sib_r.at[8 + i])
        new, wt = join(sb[w], rsb[w])
        sb[w] = new

        def cell(j, wt):
            part = pl.ds(j * HR, HR)
            blend(mb.at[w, j], rb.at[w, part], wt, base=d_b(c, w).at[part])
            return pltpu.roll(wt, 128 - HR, 1)

        lax.fori_loop(0, NZ, cell, wt)

    def a_first():
        w = zz(4)
        st = sa[w]
        usa[4] = jnp.where(lane < 2 * HR, st, NEG)
        dsa[4] = jnp.where(lane < 2 * HR, NEG, st)
        send(usa.at[4], usa.at[0], usa_s.at[0], usa_r.at[0], zup)
        send(dsa.at[4], dsa.at[0], dsa_s.at[0], dsa_r.at[0], zdn)
        for j in (0, 1):
            send(ma.at[w, j], ua.at[0, j], ua_s.at[j], ua_r.at[j], zup)
            send(ma.at[w, 2 + j], da.at[0, 2 + j], da_s.at[2 + j], da_r.at[2 + j], zdn)

    def a_step(k):
        wu, wd = zz(4 - k), zz(k - 4)
        arrived(usa.at[k - 1], usa_s.at[k - 1], usa_r.at[k - 1])
        newu, wtu = join(sa[wu], usa[k - 1])
        sa[wu] = newu
        if k < 4:
            send(sa.at[wu], usa.at[k], usa_s.at[k], usa_r.at[k], zup)
        arrived(dsa.at[k - 1], dsa_s.at[k - 1], dsa_r.at[k - 1])
        newd, wtd = join(sa[wd], dsa[k - 1])
        sa[wd] = newd
        if k < 4:
            send(sa.at[wd], dsa.at[k], dsa_s.at[k], dsa_r.at[k], zdn)

        for j in range(NY):
            n = 4 * (k - 1) + j
            if k > 1 or j < 2:
                arrived(ua.at[k - 1, j], ua_s.at[n], ua_r.at[n])
                blend(ma.at[wu, j], ua.at[k - 1, j], turned(wtu, HR * j))
            if k < 4:
                send(ma.at[wu, j], ua.at[k, j], ua_s.at[n + 4], ua_r.at[n + 4], zup)
            if k > 1 or j >= 2:
                arrived(da.at[k - 1, j], da_s.at[n], da_r.at[n])
                blend(ma.at[wd, j], da.at[k - 1, j], turned(wtd, HR * j))
            if k < 4:
                send(ma.at[wd, j], da.at[k, j], da_s.at[n + 4], da_r.at[n + 4], zdn)

    def b_first():
        w = yy(2)
        st = sb[w]
        usb[2] = jnp.where(lane < 4 * HR, st, NEG)
        dsb[2] = jnp.where(lane < 4 * HR, NEG, st)
        send(usb.at[2], usb.at[0], usb_s.at[0], usb_r.at[0], yup)
        send(dsb.at[2], dsb.at[0], dsb_s.at[0], dsb_r.at[0], ydn)
        for j in range(4):
            send(mb.at[w, j], ub.at[0, j], ub_s.at[j], ub_r.at[j], yup)
            send(mb.at[w, 4 + j], db.at[0, 4 + j], db_s.at[4 + j], db_r.at[4 + j], ydn)

    def b_step(k):
        wu, wd = yy(2 - k), yy(k - 2)
        arrived(usb.at[k - 1], usb_s.at[k - 1], usb_r.at[k - 1])
        newu, wtu = join(sb[wu], usb[k - 1])
        sb[wu] = newu
        if k < 2:
            send(sb.at[wu], usb.at[k], usb_s.at[k], usb_r.at[k], yup)
        arrived(dsb.at[k - 1], dsb_s.at[k - 1], dsb_r.at[k - 1])
        newd, wtd = join(sb[wd], dsb[k - 1])
        sb[wd] = newd
        if k < 2:
            send(sb.at[wd], dsb.at[k], dsb_s.at[k], dsb_r.at[k], ydn)
        for j in range(NZ):
            n = 8 * (k - 1) + j
            if k > 1 or j < 4:
                arrived(ub.at[k - 1, j], ub_s.at[n], ub_r.at[n])
                blend(mb.at[wu, j], ub.at[k - 1, j], turned(wtu, HR * j))
            if k < 2:
                send(mb.at[wu, j], ub.at[k, j], ub_s.at[n + 8], ub_r.at[n + 8], yup)
            if k > 1 or j >= 4:
                arrived(db.at[k - 1, j], db_s.at[n], db_r.at[n])
                blend(mb.at[wd, j], db.at[k - 1, j], turned(wtd, HR * j))
            if k < 2:
                send(mb.at[wd, j], db.at[k, j], db_s.at[n + 8], db_r.at[n + 8], ydn)

    def a_y():
        for d in (1, 2, 3):
            w = yy(d)
            send(sa.at[z], ysa.at[d - 1], ysa_s.at[d - 1], ysa_r.at[d - 1], pid(y + d, z, c))
            send(ma.at[z, w], ya.at[d - 1], ya_s.at[d - 1], ya_r.at[d - 1], pid(y + d, z, c))

    def a_y_end():
        total = turned(sa[z], HR * y)
        for d in (1, 3, 2):
            arrived(ysa.at[d - 1], ysa_s.at[d - 1], ysa_r.at[d - 1])
            total, wt = join(total, turned(ysa[d - 1], HR * y))
            arrived(ya.at[d - 1], ya_s.at[d - 1], ya_r.at[d - 1])
            blend(ma.at[z, y], ya.at[d - 1], wt)

    def bz_first():
        w = zz(4)
        usz[4] = turned(sb[y], HR * w)
        send(usz.at[4], usz.at[0], usz_s.at[0], usz_r.at[0], zup)
        send(usz.at[4], dsz.at[0], dsz_s.at[0], dsz_r.at[0], zdn)
        lo, hi = pl.ds(0, HR // 2), pl.ds(HR // 2, HR // 2)
        send(mb.at[y, w, lo], uz.at[0, lo], uz_s.at[0], uz_r.at[0], zup)
        send(mb.at[y, w, hi], dz.at[0, hi], dz_s.at[0], dz_r.at[0], zdn)

    def bz_step(k):
        wu, wd = zz(4 - k), zz(k - 4)
        lo, hi = pl.ds(0, HR // 2), pl.ds(HR // 2, HR // 2)
        arrived(usz.at[k - 1], usz_s.at[k - 1], usz_r.at[k - 1])
        ru = usz[k - 1]
        if k == 1:
            ru = jnp.where(lane < HR // 2, ru, NEG)
        newu, wtu = join(turned(sb[y], HR * wu), ru)
        if k < 4:
            usz[4 + k] = newu
            send(usz.at[4 + k], usz.at[k], usz_s.at[k], usz_r.at[k], zup)
        arrived(dsz.at[k - 1], dsz_s.at[k - 1], dsz_r.at[k - 1])
        rd = dsz[k - 1]
        if k == 1:
            rd = jnp.where(lane < HR // 2, NEG, rd)
        own = turned(sb[y], HR * wd) if k < 4 else newu
        newd, wtd = join(own, rd)
        if k < 4:
            dsz[4 + k] = newd
            send(dsz.at[4 + k], dsz.at[k], dsz_s.at[k], dsz_r.at[k], zdn)
        if k == 1:
            arrived(uz.at[0, lo], uz_s.at[0], uz_r.at[0])
            blend(mb.at[y, wu], uz.at[0], wtu, HR // 2, 0)
        else:
            arrived(uz.at[k - 1], uz_s.at[k - 1], uz_r.at[k - 1])
            blend(mb.at[y, wu], uz.at[k - 1], wtu)
        if k < 4:
            send(mb.at[y, wu], uz.at[k], uz_s.at[k], uz_r.at[k], zup)
        if k == 1:
            arrived(dz.at[0, hi], dz_s.at[0], dz_r.at[0])
            blend(mb.at[y, wd], dz.at[0], wtd, HR // 2, HR // 2)
        else:
            arrived(dz.at[k - 1], dz_s.at[k - 1], dz_r.at[k - 1])
            blend(mb.at[y, wd], dz.at[k - 1], wtd)
        if k < 4:
            send(mb.at[y, wd], dz.at[k], dz_s.at[k], dz_r.at[k], zdn)

    def share(h, cell):
        fa[...] = cell[...].astype(jnp.float32).reshape(HR * 16, HD)
        for i in range(16):
            near[h, y, :, i * HD:(i + 1) * HD] = fa[pl.ds(i, HR, stride=16), :].astype(jnp.bfloat16)
        for d in (1, 2, 3):
            n = 3 * h + d - 1
            send(near.at[h, y], near.at[h, y], n_s.at[n], n_r.at[n], pid(y + d, z, c))

    def project(h):
        for d in (1, 3, 2):
            n = 3 * h + d - 1
            arrived(near.at[h, yy(-d)], n_s.at[n], n_r.at[n])
        rows = near[h].reshape(NY * HR, near.shape[-1])
        wide = w_ref.shape[0]
        for lo in range(0, wide, 256):
            t = lax.dot_general(rows, w_ref[lo:lo + 256, :], (((1,), (1,)), ((), ())), preferred_element_type=jnp.float32)
            terms[h, :, :, lo:lo + 256] = t.astype(jnp.bfloat16).reshape(NY, HR, 256)
        for d in (1, 2, 3):
            n = 3 * h + d - 1
            to = (x + d) % NX
            send(terms.at[h, to], xin.at[h, d - 1], t_s.at[n], t_r.at[n], me, to)

    def finish(h):
        total = terms[h, x].astype(jnp.float32)
        for d in (1, 3, 2):
            n = 3 * h + d - 1
            arrived(xin.at[h, d - 1], t_s.at[n], t_r.at[n])
            total += xin[h, d - 1].astype(jnp.float32)
        tsum[h] = total.astype(jnp.bfloat16)

        @pl.when(x != y)
        def _():
            pltpu.make_async_remote_copy(src_ref=tsum.at[h], dst_ref=fin.at[h], send_sem=g_s.at[h], recv_sem=g_r.at[h], device_id=flip, device_id_type=MESH).start()

    def land(h):
        @pl.when(x != y)
        def _():
            pltpu.make_async_remote_copy(src_ref=tsum.at[h], dst_ref=fin.at[h], send_sem=g_s.at[h], recv_sem=g_r.at[h], device_id=flip, device_id_type=MESH).wait()
            out_ref[pl.ds(h * HR, HR)] = fin[h]

        @pl.when(x == y)
        def _():
            out_ref[pl.ds(h * HR, HR)] = tsum[h]

    core_a(0)
    a_first()
    core_b(0)
    b_first()
    core_a(1)
    core_a(2)
    a_step(1)
    core_b(1)
    core_b(2)
    b_step(1)
    core_a(3)
    core_a(4)
    a_step(2)
    core_a(5)
    core_a(6)
    a_step(3)
    core_b(3)
    b_step(2)
    bz_first()
    core_a(7)
    a_step(4)
    a_y()
    bz_step(1)
    bz_step(2)
    a_y_end()
    share(0, ma.at[z, y])
    bz_step(3)
    bz_step(4)
    share(1, mb.at[y, z])
    project(0)
    project(1)
    finish(0)
    finish(1)
    land(0)
    land(1)
    for d in sends:
        d.wait_send()


def merge(d, st, weight):
    dma = pltpu.SemaphoreType.DMA
    bf, f32 = jnp.bfloat16, jnp.float32

    def v(*shape, dtype=bf):
        return pltpu.VMEM(shape + (16, 128), dtype)

    anyspec = pl.BlockSpec(memory_space=pl.ANY)
    vmem = pl.BlockSpec(memory_space=pltpu.VMEM)
    sems = [6, 6, 6, 6, 2, 2]
    sems += [2, 14, 14, 16, 16, 16, 16, 4, 4, 4, 4, 16, 16, 16, 16, 2, 2, 2, 2, 3, 3, 3, 3, 4, 4, 4, 4, 4, 4, 4, 4]
    wide, deep = weight.shape
    return pl.pallas_call(
        merge_kernel,
        out_shape=jax.ShapeDtypeStruct((2 * HR, wide), bf),
        in_specs=[vmem, vmem, vmem],
        out_specs=vmem,
        scratch_shapes=[
            v(NZ, NY, HR), v(NY, NZ, HR), v(NZ, NY * HR), v(NY, NZ * HR),
            v(NZ, dtype=f32), v(NY, dtype=f32), v(NZ, dtype=f32), v(NY, dtype=f32),
            v(4, NY, HR), v(4, NY, HR), v(5, dtype=f32), v(5, dtype=f32),
            v(2, NZ, HR), v(2, NZ, HR), v(3, dtype=f32), v(3, dtype=f32),
            v(3, HR), v(3, dtype=f32),
            v(4, HR), v(4, HR), v(8, dtype=f32), v(8, dtype=f32),
            pltpu.VMEM((HR * 16, HD), f32),
            pltpu.VMEM((2, NY, HR, deep), bf),
            pltpu.VMEM((2, NY, HR, wide), bf),
            pltpu.VMEM((2, 3, HR, wide), bf),
            pltpu.VMEM((2, HR, wide), bf),
            pltpu.VMEM((2, HR, wide), bf),
        ] + [dma((n,)) for n in sems],
        compiler_params=pltpu.CompilerParams(collective_id=1, has_side_effects=True, vmem_limit_bytes=20 * 2**20),
        name="merge",
    )(d, st, pltpu.with_memory_space_constraint(weight, pltpu.VMEM))


def body(queries, span_keys, span_values, span_ids, span_slot, out_weight):
    rows, width = queries.shape
    qs, ws, last = gather(with_ids(queries.reshape(rows, width // HD, HD), span_ids), out_weight.T)
    d, st = attend(last, span_slot, qs, span_keys, span_values)
    return merge(d, st, ws.reshape(-1, width))


def solution(mesh):
    in_specs = (
        P("pool", "head"),
        P("pool", None, "head"),
        P("pool", None, "head"),
        P("pool", None),
        P(),
        P("head", "pool"),
    )
    return jax.shard_map(body, mesh=mesh, in_specs=in_specs, out_specs=P("pool", "head"), check_vma=False)
```

time: 268 us -> 148 us (0.55)
  blocking collectives: 65.5 us -> 0 us
  waiting for transfers between devices: 30.3 us -> 0 us
  between operations: 13.6 us -> 0.05 us
  Pallas kernels: 136 us -> 143 us
  local copies, waits for them, and re-layouts: 9.31 us -> 3.29 us
  matrix products: 5.22 us -> 0 us
  starting transfers between devices: 3.37 us -> 0 us
  other arithmetic: 3.87 us -> 0.79 us
    all_gather x2 -> x0, blocking collectives: 65.5 us -> none  [the longest x1 52.8 us: body(): ids_all = lax.all_gather(span_ids, 'pool', axis=0, tiled=True)]
    reduce_scatter x1 -> x0, waiting for transfers between devices: 22.4 us -> none  [body(): lax.psum_scatter(terms.astype(jnp.bfloat16), 'head', scatter_dimension=0,...]
    ppermute x1 -> x0, waiting for transfers between devices: 7.2 us -> none  [body(): return lax.ppermute(mine, ('pool', 'head'), perm)]
    pallas_call x3, Pallas kernels: 136 us -> 143 us  [the longest x1 66 us: merge(): pl.pallas_call(merge_kernel, out_shape=jax.ShapeDtypeStruct((2 * HR, wide...]
    dot_general x2 -> x0, matrix products: 5.22 us -> none  [the longest x1 5.08 us: body(): lax.dot_general(near, weight, (((1,), (1,)), ((), ())), preferred_element...]
    unnamed x16 -> x6, local copies, waits for them, and re-layouts: 7.56 us -> 3.21 us
    ppermute x1 -> x0, starting transfers between devices: 3.33 us -> none  [body(): return lax.ppermute(mine, ('pool', 'head'), perm)]
    reduce_sum x5 -> x0, other arithmetic: 3.22 us -> none  [the longest x1 1.22 us: span_lists(): jnp.sum(jnp.where(rank[:, None, :] == slot[None, :, None], place[:, None,...]
  transfers between devices with their start and end apart: 3 -> 0, of which waited for: 2 -> 0; matrix products, arithmetic and copies ran while one was open for 3% -> 0% of each run, Pallas kernels for 51% -> 0%
where the time goes in v2:
time: 148 us
  Pallas kernels  143 us (97%)
  local copies, waits for them, and re-layouts  3.29 us (2%)
    pallas_call x1, Pallas kernels, merge(): pl.pallas_call(merge_kernel, out_shape=jax.ShapeDtypeStruct((2 * HR, wide...  66 us
    pallas_call x1, Pallas kernels, gather(): pl.pallas_call(gather_kernel, out_shape=(pltpu.VMEM((NC, NY, NZ) + q.shap...  50.3 us
    pallas_call x1, Pallas kernels, attend(): pl.pallas_call(attend_kernel, out_shape=(pltpu.VMEM((ROWS + 8, 16, HD), j...  27.2 us
    unnamed x6, local copies, waits for them, and re-layouts  3.21 us

profile of v2, /device:TPU:16, one launch (start us, length us, event | category | flops | bytes accessed | tf_op | source)
XLA Modules:
  0.0 147.6 jit_solution(8993934492144707234)
XLA Ops:
  0.0 0.7 fusion.6
  0.7 0.1 pad.3.clone
  0.8 0.9 copy.7
  1.7 0.1 maximum_maximum_fusion.q_ref
  1.8 0.0 copy-start
  1.8 1.0 copy-done
  2.8 50.3 %gather.1 = (bf16[2,4,8,33,16,128]{5,4,3,2,1,0:T(8,128)(2,1)S(1)}, bf16[8,2,80,2048]{3,2,1,0:T(8,128)(2,1)S(1)}, bf16[2,4,8,16,128]{4,3,2,1,0:T(8,128)(2,1)S(1)}) custom-call(bf16[33,16,128]{2,1,0:T(8,128)(2,1)S(1)} %maximum_maximum_fusion.q_ref, bf16[80,2048]{1,0:T(8,128)(2,1)S(1)} %bitcast.43), custom_call_target="tpu_custom_call" | custom-call | tf_op jit(solution)/shard_map/gather/pallas_call | solution.py:187
  53.1 0.0 copy-start.1
  53.1 0.7 copy-done.1
  53.8 27.2 %attend.1 = (bf16[2056,16,128]{2,1,0:T(8,128)(2,1)S(1)}, f32[25,16,128]{2,1,0:T(8,128)S(1)}) custom-call(bf16[64,16,128]{2,1,0:T(8,128)(2,1)S(1)} %bitcast.44, s32[4,128]{1,0:T(4,128)S(1)} %bitcast.45, bf16[2112,16,128]{2,1,0:T(8,128)(2,1)S(1)} %bitcast.41, bf16[8,512,256]{2,1,0:T(8,128)(2,1)} %k_hbm.1, bf16[8,512,256]{2,1,0:T(8,128)(2,1)} %v_hbm.1), custom_call_target="tpu_custom_call" | custom-call | tf_op jit(solution)/shard_map/attend/pallas_call | solution.py:349
  81.0 66.0 %merge.1 = bf16[32,1280]{1,0:T(8,128)(2,1)S(1)} custom-call(bf16[2056,16,128]{2,1,0:T(8,128)(2,1)S(1)} %get-tuple-element.12.d_ref, f32[25,16,128]{2,1,0:T(8,128)S(1)} %get-tuple-element.13.st_ref, bf16[1280,2048]{1,0:T(8,128)(2,1)S(1)} %bitcast.42), custom_call_target="tpu_custom_call" | custom-call | tf_op jit(solution)/shard_map/merge/pallas_call | solution.py:736
  147.0 0.6 copy.9
  (1 shorter events, 0.0 us)
Async XLA Ops:
  1.8 1.0 copy-start
  53.1 0.7 copy-start.1

commit v3 on v2

--- a/solution.py
+++ b/solution.py
@@ -200,8 +200,8 @@
 
 
 NEG = -1e30
-CHUNK = 32
-BATCH = 8
+CHUNK = 64
+BATCH = 32
 ROWS = 2048
 GROUPS = 24
 
@@ -214,7 +214,7 @@
 
 
 def list_requests(last_ref, slot_ref, first_ref, second_ref, lists_ref, counts_ref):
-    spans = lists_ref.shape[0]
+    spans = counts_ref.shape[0]
     me = lax.axis_index("pool")
     slots = slot_ref[...]
     where_id = lax.broadcasted_iota(jnp.int32, slots.shape, 0) * 128 + lax.broadcasted_iota(jnp.int32, slots.shape, 1)
@@ -263,6 +263,7 @@
             place = jnp.where(r < HR, early, late) + r + 4096 * (b * 33 + r)
             listing += jnp.sum(jnp.where(used & (rank == k), place, 0), axis=0, keepdims=True)
             count += jnp.sum(one, axis=0, keepdims=True)
+        lists_ref[spans:spans + 8, :] = jnp.full((8, 128), ROWS, jnp.int32)
         lists_ref[s:s + 1, :] = jnp.where(lane[0:1].astype(jnp.float32) < count, listing, ROWS)
         counts_ref[s:s + 1, :] = count.astype(jnp.int32)
 
@@ -290,54 +291,69 @@
     scale2 = math.log2(math.e) / math.sqrt(HD)
     lane = lax.broadcasted_iota(jnp.int32, (16, 128), 1)
 
-    def span(s, _):
-        pltpu.make_async_copy(k_hbm.at[s], kbuf.at[s], ksem.at[s]).wait()
-        pltpu.make_async_copy(v_hbm.at[s], vbuf.at[s], vsem.at[s]).wait()
-        n = count_ref[s, 0]
-
-        def chunk(j, _):
-            base = j * CHUNK
-            for i in range(0, CHUNK, 2):
-                a = q_ref[list_ref[s, base + i] >> 12].astype(jnp.float32)
-                b = q_ref[list_ref[s, base + i + 1] >> 12].astype(jnp.float32)
-                l0[pl.ds(i * 8, 16)] = jnp.concatenate([a[0:8], b[0:8]], axis=0).astype(jnp.bfloat16)
-                l1[pl.ds(i * 8, 16)] = jnp.concatenate([a[8:16], b[8:16]], axis=0).astype(jnp.bfloat16)
-            for kv, (l, p, e) in enumerate(((l0, p0, e0), (l1, p1, e1))):
-                keys = kbuf[s, :, kv * HD:(kv + 1) * HD]
-                vals = vbuf[s, :, kv * HD:(kv + 1) * HD]
-                sc = lax.dot_general(l[...], keys, (((1,), (1,)), ((), ())), preferred_element_type=jnp.float32) * scale2
-                m = jnp.max(sc, axis=1, keepdims=True)
-                ex = jnp.exp2(sc - m)
-                tot = jnp.sum(ex, axis=1, keepdims=True)
-                pv = jnp.dot(ex.astype(jnp.bfloat16), vals, preferred_element_type=jnp.float32)
-                p[...] = pv / tot
-                e[...] = jnp.broadcast_to(m + jnp.log2(tot), e.shape)
-            for first in range(0, CHUNK, BATCH):
-                done = []
-                for i in range(first, first + BATCH):
-                    place = list_ref[s, base + i] & 4095
-                    early = place < ROWS // 2
-                    g = jnp.where(early, place >> 6, 8 + (place >> 7))
-                    at = place & jnp.where(early, 63, 127)
-                    here = lane == at
-                    new = jnp.concatenate([p0[pl.ds(i * 8, 8)], p1[pl.ds(i * 8, 8)]], axis=0)
-                    le = jnp.concatenate([e0[pl.ds(i * 8, 8)], e1[pl.ds(i * 8, 8)]], axis=0)
-                    old = d_ref[place].astype(jnp.float32)
-                    ol = jnp.max(jnp.where(here, st_ref[g], -3e38), axis=1, keepdims=True)
-                    ex = jnp.exp2(-jnp.abs(le - ol))
-                    both = 1.0 + ex
-                    w = jnp.where(le > ol, 1.0, ex) / both
-                    done.append((place, g, here, old + w * (new - old), jnp.maximum(le, ol) + jnp.log2(both)))
-                for place, g, here, tile, le in done:
-                    d_ref[place] = tile.astype(jnp.bfloat16)
-                for place, g, here, tile, le in done:
-                    st_ref[g] = jnp.where(here, le, st_ref[g])
-            return 0
-
-        lax.fori_loop(0, (n + CHUNK - 1) // CHUNK, chunk, 0)
-        return 0
-
-    lax.fori_loop(0, spans, span, 0)
+    def compute(s, base, slot):
+        for i in range(0, CHUNK, 2):
+            a = q_ref[list_ref[s, base + i] >> 12].astype(jnp.float32)
+            b = q_ref[list_ref[s, base + i + 1] >> 12].astype(jnp.float32)
+            l0[pl.ds(i * 8, 16)] = jnp.concatenate([a[0:8], b[0:8]], axis=0).astype(jnp.bfloat16)
+            l1[pl.ds(i * 8, 16)] = jnp.concatenate([a[8:16], b[8:16]], axis=0).astype(jnp.bfloat16)
+        scores = []
+        for kv, l in enumerate((l0, l1)):
+            keys = kbuf[s, :, kv * HD:(kv + 1) * HD]
+            scores.append(lax.dot_general(l[...], keys, (((1,), (1,)), ((), ())), preferred_element_type=jnp.float32) * scale2)
+        for kv, (p, e) in enumerate(((p0, e0), (p1, e1))):
+            sc = scores[kv]
+            vals = vbuf[s, :, kv * HD:(kv + 1) * HD]
+            m = jnp.max(sc, axis=1, keepdims=True)
+            ex = jnp.exp2(sc - m)
+            tot = jnp.sum(ex, axis=1, keepdims=True)
+            pv = jnp.dot(ex.astype(jnp.bfloat16), vals, preferred_element_type=jnp.float32)
+            p[slot] = pv * (1.0 / tot)
+            e[slot] = jnp.broadcast_to(m + jnp.log2(tot), e.shape[1:])
+
+    def fold(s, base, slot):
+        for first in range(0, CHUNK, BATCH):
+            done = []
+            for i in range(first, first + BATCH):
+                place = list_ref[s, base + i] & 4095
+                early = place < ROWS // 2
+                g = jnp.where(early, place >> 6, 8 + (place >> 7))
+                at = place & jnp.where(early, 63, 127)
+                here = lane == at
+                new = jnp.concatenate([p0[slot, pl.ds(i * 8, 8)], p1[slot, pl.ds(i * 8, 8)]], axis=0)
+                le = jnp.concatenate([e0[slot, pl.ds(i * 8, 8)], e1[slot, pl.ds(i * 8, 8)]], axis=0)
+                old = d_ref[place].astype(jnp.float32)
+                ol = jnp.max(jnp.where(here, st_ref[g], -3e38), axis=1, keepdims=True)
+                ex = jnp.exp2(-jnp.abs(le - ol))
+                both = 1.0 + ex
+                w = jnp.where(le > ol, 1.0, ex) / both
+                done.append((place, g, here, old + w * (new - old), jnp.maximum(le, ol) + jnp.log2(both)))
+            for place, g, here, tile, le in done:
+                d_ref[place] = tile.astype(jnp.bfloat16)
+            for place, g, here, tile, le in done:
+                st_ref[g] = jnp.where(here, le, st_ref[g])
+
+    total = jnp.int32(0)
+    for s in range(spans):
+        total += jnp.maximum((count_ref[s, 0] + CHUNK - 1) // CHUNK, 1)
+
+    def step(t, carry):
+        s, base, s_before, base_before = carry
+
+        @pl.when(base == 0)
+        def _():
+            pltpu.make_async_copy(k_hbm.at[s], kbuf.at[s], ksem.at[s]).wait()
+            pltpu.make_async_copy(v_hbm.at[s], vbuf.at[s], vsem.at[s]).wait()
+
+        slot = t % 2
+        compute(s, base, slot)
+        fold(s_before, base_before, 1 - slot)
+        more = base + CHUNK < count_ref[s, 0]
+        return jnp.where(more, s, s + 1), jnp.where(more, base + CHUNK, 0), s, base
+
+    zero = jnp.int32(0)
+    _, _, s, base = lax.fori_loop(0, total, step, (zero, zero, jnp.int32(spans), zero))
+    fold(s, base, (total - 1) % 2)
 
 
 def attend(last, span_slot, qs, span_keys, span_values):
@@ -352,12 +368,12 @@
         in_specs=[vmem, vmem, vmem, anyspec, anyspec],
         out_specs=(vmem, vmem),
         scratch_shapes=[pltpu.VMEM((blocks * 8, 128), jnp.float32)] * 2
-        + [pltpu.VMEM((spans, 128), jnp.int32)] * 2
-        + [pltpu.SMEM((spans, 128), jnp.int32)] * 2
+        + [pltpu.VMEM((spans + 8, 128), jnp.int32), pltpu.VMEM((spans, 128), jnp.int32)]
+        + [pltpu.SMEM((spans + 8, 128), jnp.int32), pltpu.SMEM((spans, 128), jnp.int32)]
         + [pltpu.SemaphoreType.DMA((2,))]
         + [pltpu.VMEM(span_keys.shape, jnp.bfloat16)] * 2
         + [pltpu.VMEM((rows, HD), jnp.bfloat16)] * 2
-        + [pltpu.VMEM((rows, HD), jnp.float32)] * 4
+        + [pltpu.VMEM((2, rows, HD), jnp.float32)] * 4
         + [pltpu.SemaphoreType.DMA((spans,))] * 2,
         compiler_params=pltpu.CompilerParams(vmem_limit_bytes=24 * 2**20),
         name="attend",
@@ -505,21 +521,25 @@
 
         lax.fori_loop(0, NZ, cell, wt)
 
+    a_up, a_dn = (2, 3, 0, 1), (0, 1, 2, 3)
+    a_wt = {}
+
     def a_first():
         w = zz(4)
+        for i in (0, 1):
+            send(ma.at[w, i], ua.at[0, i], ua_s.at[i], ua_r.at[i], zup)
+            send(ma.at[w, 2 + i], da.at[0, 2 + i], da_s.at[2 + i], da_r.at[2 + i], zdn)
         st = sa[w]
         usa[4] = jnp.where(lane < 2 * HR, st, NEG)
         dsa[4] = jnp.where(lane < 2 * HR, NEG, st)
         send(usa.at[4], usa.at[0], usa_s.at[0], usa_r.at[0], zup)
         send(dsa.at[4], dsa.at[0], dsa_s.at[0], dsa_r.at[0], zdn)
-        for j in (0, 1):
-            send(ma.at[w, j], ua.at[0, j], ua_s.at[j], ua_r.at[j], zup)
-            send(ma.at[w, 2 + j], da.at[0, 2 + j], da_s.at[2 + j], da_r.at[2 + j], zdn)
-
-    def a_step(k):
+
+    def a_stat(k):
         wu, wd = zz(4 - k), zz(k - 4)
         arrived(usa.at[k - 1], usa_s.at[k - 1], usa_r.at[k - 1])
-        newu, wtu = join(sa[wu], usa[k - 1])
+        own = sa[wu]
+        newu, wtu = join(own, usa[k - 1])
         sa[wu] = newu
         if k < 4:
             send(sa.at[wu], usa.at[k], usa_s.at[k], usa_r.at[k], zup)
@@ -528,35 +548,45 @@
         sa[wd] = newd
         if k < 4:
             send(sa.at[wd], dsa.at[k], dsa_s.at[k], dsa_r.at[k], zdn)
-
-        for j in range(NY):
+        if k == 4:
+            early, wtd1 = join(own, dsa[k - 1])
+            _, wtu2 = join(early, usa[k - 1])
+            wtu = jnp.where(lane < 2 * HR, wtu2, wtu)
+            wtd = jnp.where(lane < 2 * HR, wtd1, wtd)
+        a_wt[k] = (wtu, wtd)
+
+    def a_cell(k, i):
+        wu, wd = zz(4 - k), zz(k - 4)
+        for j, w, buf, ss, rs, to, t, has in (
+            (a_up[i], wu, ua, ua_s, ua_r, zup, 0, k > 1 or a_up[i] < 2),
+            (a_dn[i], wd, da, da_s, da_r, zdn, 1, k > 1 or a_dn[i] >= 2),
+        ):
             n = 4 * (k - 1) + j
-            if k > 1 or j < 2:
-                arrived(ua.at[k - 1, j], ua_s.at[n], ua_r.at[n])
-                blend(ma.at[wu, j], ua.at[k - 1, j], turned(wtu, HR * j))
+            if has:
+                arrived(buf.at[k - 1, j], ss.at[n], rs.at[n])
+                blend(ma.at[w, j], buf.at[k - 1, j], turned(a_wt[k][t], HR * j))
             if k < 4:
-                send(ma.at[wu, j], ua.at[k, j], ua_s.at[n + 4], ua_r.at[n + 4], zup)
-            if k > 1 or j >= 2:
-                arrived(da.at[k - 1, j], da_s.at[n], da_r.at[n])
-                blend(ma.at[wd, j], da.at[k - 1, j], turned(wtd, HR * j))
-            if k < 4:
-                send(ma.at[wd, j], da.at[k, j], da_s.at[n + 4], da_r.at[n + 4], zdn)
+                send(ma.at[w, j], buf.at[k, j], ss.at[n + 4], rs.at[n + 4], to)
+
+    b_up, b_dn = (4, 5, 6, 7, 0, 1, 2, 3), (0, 1, 2, 3, 4, 5, 6, 7)
+    b_wt = {}
 
     def b_first():
         w = yy(2)
+        for j in range(4):
+            send(mb.at[w, j], ub.at[0, j], ub_s.at[j], ub_r.at[j], yup)
+            send(mb.at[w, 4 + j], db.at[0, 4 + j], db_s.at[4 + j], db_r.at[4 + j], ydn)
         st = sb[w]
         usb[2] = jnp.where(lane < 4 * HR, st, NEG)
         dsb[2] = jnp.where(lane < 4 * HR, NEG, st)
         send(usb.at[2], usb.at[0], usb_s.at[0], usb_r.at[0], yup)
         send(dsb.at[2], dsb.at[0], dsb_s.at[0], dsb_r.at[0], ydn)
-        for j in range(4):
-            send(mb.at[w, j], ub.at[0, j], ub_s.at[j], ub_r.at[j], yup)
-            send(mb.at[w, 4 + j], db.at[0, 4 + j], db_s.at[4 + j], db_r.at[4 + j], ydn)
-
-    def b_step(k):
+
+    def b_stat(k):
         wu, wd = yy(2 - k), yy(k - 2)
         arrived(usb.at[k - 1], usb_s.at[k - 1], usb_r.at[k - 1])
-        newu, wtu = join(sb[wu], usb[k - 1])
+        own = sb[wu]
+        newu, wtu = join(own, usb[k - 1])
         sb[wu] = newu
         if k < 2:
             send(sb.at[wu], usb.at[k], usb_s.at[k], usb_r.at[k], yup)
@@ -565,18 +595,25 @@
         sb[wd] = newd
         if k < 2:
             send(sb.at[wd], dsb.at[k], dsb_s.at[k], dsb_r.at[k], ydn)
-        for j in range(NZ):
+        if k == 2:
+            early, wtd1 = join(own, dsb[k - 1])
+            _, wtu2 = join(early, usb[k - 1])
+            wtu = jnp.where(lane < 4 * HR, wtu2, wtu)
+            wtd = jnp.where(lane < 4 * HR, wtd1, wtd)
+        b_wt[k] = (wtu, wtd)
+
+    def b_cell(k, i):
+        wu, wd = yy(2 - k), yy(k - 2)
+        for j, w, buf, ss, rs, to, t, has in (
+            (b_up[i], wu, ub, ub_s, ub_r, yup, 0, k > 1 or b_up[i] < 4),
+            (b_dn[i], wd, db, db_s, db_r, ydn, 1, k > 1 or b_dn[i] >= 4),
+        ):
             n = 8 * (k - 1) + j
-            if k > 1 or j < 4:
-                arrived(ub.at[k - 1, j], ub_s.at[n], ub_r.at[n])
-                blend(mb.at[wu, j], ub.at[k - 1, j], turned(wtu, HR * j))
+            if has:
+                arrived(buf.at[k - 1, j], ss.at[n], rs.at[n])
+                blend(mb.at[w, j], buf.at[k - 1, j], turned(b_wt[k][t], HR * j))
             if k < 2:
-                send(mb.at[wu, j], ub.at[k, j], ub_s.at[n + 8], ub_r.at[n + 8], yup)
-            if k > 1 or j >= 4:
-                arrived(db.at[k - 1, j], db_s.at[n], db_r.at[n])
-                blend(mb.at[wd, j], db.at[k - 1, j], turned(wtd, HR * j))
-            if k < 2:
-                send(mb.at[wd, j], db.at[k, j], db_s.at[n + 8], db_r.at[n + 8], ydn)
+                send(mb.at[w, j], buf.at[k, j], ss.at[n + 8], rs.at[n + 8], to)
 
     def a_y():
         for d in (1, 2, 3):
@@ -688,23 +725,39 @@
     b_first()
     core_a(1)
     core_a(2)
-    a_step(1)
+    a_cell(1, 0)
+    a_cell(1, 1)
     core_b(1)
     core_b(2)
-    b_step(1)
+    for i in range(4):
+        b_cell(1, i)
+    a_stat(1)
+    a_cell(1, 2)
+    a_cell(1, 3)
     core_a(3)
     core_a(4)
-    a_step(2)
+    b_stat(1)
+    a_stat(2)
+    for i in range(4):
+        a_cell(2, i)
+        b_cell(1, 4 + i)
     core_a(5)
     core_a(6)
-    a_step(3)
+    a_stat(3)
     core_b(3)
-    b_step(2)
-    bz_first()
+    b_stat(2)
+    for i in range(4):
+        a_cell(3, i)
+        b_cell(2, i)
     core_a(7)
-    a_step(4)
+    a_stat(4)
+    for i in range(4):
+        b_cell(2, 4 + i)
+        if i == 3:
+            bz_first()
+        a_cell(4, i)
+    bz_step(1)
     a_y()
-    bz_step(1)
     bz_step(2)
     a_y_end()
     share(0, ma.at[z, y])

time: 148 us -> 137 us (0.926)
  Pallas kernels: 143 us -> 133 us
    pallas_call x1, Pallas kernels: 27.2 us -> 19.5 us  [attend(): pl.pallas_call(attend_kernel, out_shape=(pltpu.VMEM((ROWS + 8, 16, HD), j...]
    pallas_call x1, Pallas kernels: 66 us -> 63.4 us  [merge(): pl.pallas_call(merge_kernel, out_shape=jax.ShapeDtypeStruct((2 * HR, wide...]
where the time goes in v3:
time: 137 us
  Pallas kernels  133 us (97%)
  local copies, waits for them, and re-layouts  3.29 us (2%)
    pallas_call x1, Pallas kernels, merge(): pl.pallas_call(merge_kernel, out_shape=jax.ShapeDtypeStruct((2 * HR, wide...  63.4 us
    pallas_call x1, Pallas kernels, gather(): pl.pallas_call(gather_kernel, out_shape=(pltpu.VMEM((NC, NY, NZ) + q.shap...  50.3 us
    pallas_call x1, Pallas kernels, attend(): pl.pallas_call(attend_kernel, out_shape=(pltpu.VMEM((ROWS + 8, 16, HD), j...  19.5 us
    unnamed x6, local copies, waits for them, and re-layouts  3.21 us

profile of v3, /device:TPU:16, one launch (start us, length us, event | category | flops | bytes accessed | tf_op | source)
XLA Modules:
  0.0 137.3 jit_solution(15739208045398977048)
XLA Ops:
  0.0 0.7 fusion.6
  0.7 0.1 pad.3.clone
  0.8 0.9 copy.7
  1.7 0.1 maximum_maximum_fusion.q_ref
  1.8 0.0 copy-start
  1.8 1.0 copy-done
  2.8 50.3 %gather.1 = (bf16[2,4,8,33,16,128]{5,4,3,2,1,0:T(8,128)(2,1)S(1)}, bf16[8,2,80,2048]{3,2,1,0:T(8,128)(2,1)S(1)}, bf16[2,4,8,16,128]{4,3,2,1,0:T(8,128)(2,1)S(1)}) custom-call(bf16[33,16,128]{2,1,0:T(8,128)(2,1)S(1)} %maximum_maximum_fusion.q_ref, bf16[80,2048]{1,0:T(8,128)(2,1)S(1)} %bitcast.43), custom_call_target="tpu_custom_call" | custom-call | tf_op jit(solution)/shard_map/gather/pallas_call | solution.py:187
  53.1 0.0 copy-start.1
  53.1 0.7 copy-done.1
  53.8 19.5 %attend.1 = (bf16[2056,16,128]{2,1,0:T(8,128)(2,1)S(1)}, f32[25,16,128]{2,1,0:T(8,128)S(1)}) custom-call(bf16[64,16,128]{2,1,0:T(8,128)(2,1)S(1)} %bitcast.44, s32[4,128]{1,0:T(4,128)S(1)} %bitcast.45, bf16[2112,16,128]{2,1,0:T(8,128)(2,1)S(1)} %bitcast.41, bf16[8,512,256]{2,1,0:T(8,128)(2,1)} %k_hbm.1, bf16[8,512,256]{2,1,0:T(8,128)(2,1)} %v_hbm.1), custom_call_target="tpu_custom_call" | custom-call | tf_op jit(solution)/shard_map/attend/pallas_call | solution.py:365
  73.2 63.4 %merge.1 = bf16[32,1280]{1,0:T(8,128)(2,1)S(1)} custom-call(bf16[2056,16,128]{2,1,0:T(8,128)(2,1)S(1)} %get-tuple-element.12.d_ref, f32[25,16,128]{2,1,0:T(8,128)S(1)} %get-tuple-element.13.st_ref, bf16[1280,2048]{1,0:T(8,128)(2,1)S(1)} %bitcast.42), custom_call_target="tpu_custom_call" | custom-call | tf_op jit(solution)/shard_map/merge/pallas_call | solution.py:789
  136.7 0.6 copy.9
  (1 shorter events, 0.0 us)
Async XLA Ops:
  1.8 1.0 copy-start
  53.1 0.7 copy-start.1

commit v4 on v3

--- a/solution.py
+++ b/solution.py
@@ -196,7 +196,7 @@
         scratch_shapes=[dma((n,)) for n in (2, 8, 8, 16, 16, 16, 16, 32, 32, 8, 8, 8, 8)],
         compiler_params=pltpu.CompilerParams(collective_id=0, has_side_effects=True, vmem_limit_bytes=2**20),
         name="gather",
-    )(q, wt)
+    )(q, pltpu.with_memory_space_constraint(wt, pltpu.HBM))
 
 
 NEG = -1e30
@@ -683,19 +683,21 @@
             n = 3 * h + d - 1
             send(near.at[h, y], near.at[h, y], n_s.at[n], n_r.at[n], pid(y + d, z, c))
 
-    def project(h):
-        for d in (1, 3, 2):
-            n = 3 * h + d - 1
-            arrived(near.at[h, yy(-d)], n_s.at[n], n_r.at[n])
-        rows = near[h].reshape(NY * HR, near.shape[-1])
+    def project():
+        for h in (0, 1):
+            for d in (1, 3, 2):
+                n = 3 * h + d - 1
+                arrived(near.at[h, yy(-d)], n_s.at[n], n_r.at[n])
+        rows = near[...].reshape(2 * NY * HR, near.shape[-1])
         wide = w_ref.shape[0]
         for lo in range(0, wide, 256):
             t = lax.dot_general(rows, w_ref[lo:lo + 256, :], (((1,), (1,)), ((), ())), preferred_element_type=jnp.float32)
-            terms[h, :, :, lo:lo + 256] = t.astype(jnp.bfloat16).reshape(NY, HR, 256)
-        for d in (1, 2, 3):
-            n = 3 * h + d - 1
-            to = (x + d) % NX
-            send(terms.at[h, to], xin.at[h, d - 1], t_s.at[n], t_r.at[n], me, to)
+            terms[:, :, :, lo:lo + 256] = t.astype(jnp.bfloat16).reshape(2, NY, HR, 256)
+        for h in (0, 1):
+            for d in (1, 2, 3):
+                n = 3 * h + d - 1
+                to = (x + d) % NX
+                send(terms.at[h, to], xin.at[h, d - 1], t_s.at[n], t_r.at[n], me, to)
 
     def finish(h):
         total = terms[h, x].astype(jnp.float32)
@@ -764,8 +766,7 @@
     bz_step(3)
     bz_step(4)
     share(1, mb.at[y, z])
-    project(0)
-    project(1)
+    project()
     finish(0)
     finish(1)
     land(0)

time: 137 us -> 138 us (level); the launches traced: 137 us -> 137 us
    pallas_call x1, Pallas kernels: 63.4 us -> 65.1 us  [merge(): pl.pallas_call(merge_kernel, out_shape=jax.ShapeDtypeStruct((2 * HR, wide...]
    pallas_call x1, Pallas kernels: 19.5 us -> 18 us  [attend(): pl.pallas_call(attend_kernel, out_shape=(pltpu.VMEM((ROWS + 8, 16, HD), j...]
    unnamed x6 -> x4, local copies, waits for them, and re-layouts: 3.21 us -> 2.24 us
where the time goes in v4:
time: 138 us; the launch traced here: 137 us
  Pallas kernels  133 us (96%)
  local copies, waits for them, and re-layouts  2.32 us (2%)
    pallas_call x1, Pallas kernels, merge(): pl.pallas_call(merge_kernel, out_shape=jax.ShapeDtypeStruct((2 * HR, wide...  65.1 us
    pallas_call x1, Pallas kernels, gather(): pl.pallas_call(gather_kernel, out_shape=(pltpu.VMEM((NC, NY, NZ) + q.shap...  50.3 us
    pallas_call x1, Pallas kernels, attend(): pl.pallas_call(attend_kernel, out_shape=(pltpu.VMEM((ROWS + 8, 16, HD), j...  18 us

profile of v4, /device:TPU:16, one launch (start us, length us, event | category | flops | bytes accessed | tf_op | source)
XLA Modules:
  0.0 136.6 jit_solution(15112137562445182991)
XLA Ops:
  0.0 0.7 fusion.6
  0.7 0.1 pad.3.clone
  0.8 0.9 copy.7
  1.7 0.1 maximum_maximum_fusion.q_ref
  1.8 50.3 %gather.1 = (bf16[2,4,8,33,16,128]{5,4,3,2,1,0:T(8,128)(2,1)S(1)}, bf16[8,2,80,2048]{3,2,1,0:T(8,128)(2,1)S(1)}, bf16[2,4,8,16,128]{4,3,2,1,0:T(8,128)(2,1)S(1)}) custom-call(bf16[33,16,128]{2,1,0:T(8,128)(2,1)S(1)} %maximum_maximum_fusion.q_ref, bf16[80,2048]{1,0:T(8,128)(2,1)} %bitcast.46), custom_call_target="tpu_custom_call" | custom-call | tf_op jit(solution)/shard_map/gather/pallas_call | solution.py:187
  52.2 0.0 copy-start
  52.2 0.7 copy-done
  52.9 18.0 %attend.1 = (bf16[2056,16,128]{2,1,0:T(8,128)(2,1)S(1)}, f32[25,16,128]{2,1,0:T(8,128)S(1)}) custom-call(bf16[64,16,128]{2,1,0:T(8,128)(2,1)S(1)} %bitcast.43, s32[4,128]{1,0:T(4,128)S(1)} %bitcast.44, bf16[2112,16,128]{2,1,0:T(8,128)(2,1)S(1)} %bitcast.41, bf16[8,512,256]{2,1,0:T(8,128)(2,1)} %k_hbm.1, bf16[8,512,256]{2,1,0:T(8,128)(2,1)} %v_hbm.1), custom_call_target="tpu_custom_call" | custom-call | tf_op jit(solution)/shard_map/attend/pallas_call | solution.py:365
  70.8 65.1 %merge.1 = bf16[32,1280]{1,0:T(8,128)(2,1)S(1)} custom-call(bf16[2056,16,128]{2,1,0:T(8,128)(2,1)S(1)} %get-tuple-element.12.d_ref, f32[25,16,128]{2,1,0:T(8,128)S(1)} %get-tuple-element.13.st_ref, bf16[1280,2048]{1,0:T(8,128)(2,1)S(1)} %bitcast.42), custom_call_target="tpu_custom_call" | custom-call | tf_op jit(solution)/shard_map/merge/pallas_call | solution.py:790
  136.0 0.6 copy.9
  (1 shorter events, 0.0 us)
Async XLA Ops:
  52.2 0.7 copy-start
